TPU v7x, 32 devices: a whole 2x2x4 slice. The times are simulated.
32 devices in a mesh: groups: 2 (over x), lat: 8 (over z, y), lon: 2 (over core).
Axes of the slice: x: 2, y: 2, z: 4, core: 2. Of those that a mesh axis runs over, the one named last changes fastest.
Arguments:
- state_field: bfloat16 [64, 1440, 256], P(('groups', 'lat'), 'lon'), parts along dimension 0, may hold values from -6 to 6
- heights: int32 [16], P(('groups', 'lat')), parts along dimension 0, may hold values from 1 to 4, 16 in all
- halo_widths: int32 [64], P(('groups', 'lat')), parts along dimension 0, may hold values from 1 to 8, as said below
- filter_values: bfloat16 [64, 3, 3, 17], P(('groups', 'lat')), parts along dimension 0, may hold values from -1.1953125 to 1.1953125
- weights_one: bfloat16 [3, 256, 256], replicated, may hold values from -0.21875 to 0.21875
- weights_two: bfloat16 [3, 256, 256], replicated, may hold values from -0.21875 to 0.21875
- cotangent: bfloat16 [64, 1440, 256], P(('groups', 'lat'), 'lon'), parts along dimension 0, may hold values from -6 to 6
Outputs:
- next_field: bfloat16 [64, 1440, 256], P(('groups', 'lat'), 'lon'), parts along dimension 0
- grad_field: bfloat16 [64, 1440, 256], P(('groups', 'lat'), 'lon'), parts along dimension 0
- grad_weights_one: float32 [6, 256, 256], P('groups'), parts along dimension 0
- grad_weights_two: float32 [6, 256, 256], P('groups'), parts along dimension 0
There are 2 independent parts, one for each index of `groups`. A program takes and returns all parts, laid end to end along the dimension named above; an argument that names none is the same for every part. Nothing has to cross between parts.
Inputs may be any that keep to these rules, and one draw needn't show every extreme that they name: `heights`: the entries sum to 16 and one of them equals 4. `halo_widths`: slot 0 holds 8; values in slots that are not live are unused.
All inputs are finite; a program needn't handle non-finite values. No bound on the sum of `heights` on one device may be relied on, other than what follows from the above.
Results may differ from a plain program's by a relative error of at most 0.007.
Values may be sent and summed in bfloat16 or wider, within the bound.
No kernel may reach another device: no remote copies, remote signals or barrier semaphores. Data moves between devices by JAX's collectives and lax.ppermute only.
A program may use at most 64 MiB of HBM per device.

v0:
```python
import math

import jax
import jax.numpy as jnp
from jax import lax
from jax.sharding import PartitionSpec as P

NLON = 1440
HALO = 8
ROWS = 2


def shifted(block, axis, distance):
    devices = range(lax.axis_size(axis))
    route = [(i - distance, i) for i in devices if i - distance in devices]
    return lax.ppermute(block, axis, route)


def padded_2(value, sides, width):
    for axis, dim in sides:
        size, length = (lax.axis_size(axis), value.shape[dim])
        up = [(i, (i + 1) % size) for i in range(size)]
        down = [(j, i) for i, j in up]
        last = lax.slice_in_dim(value, length - width, length, axis=dim)
        leading = lax.slice_in_dim(value, 0, width, axis=dim)
        before = lax.ppermute(last, axis, up)
        after = lax.ppermute(leading, axis, down)
        value = jnp.concatenate([before, value, after], axis=dim)
    return value


def gelu_slope(values):
    inner = 0.5 * (1.0 + jax.scipy.special.erf(values * (1.0 / math.sqrt(2.0))))
    return inner + values * jnp.exp(-0.5 * values * values) * (1.0 / math.sqrt(2.0 * math.pi))


def masked_filter(filter_values, halo_widths):
    span_count = filter_values.shape[-1]
    offsets = jnp.abs(jnp.arange(span_count, dtype=jnp.int32) - (span_count - 1) // 2)
    inside = offsets[None, :] <= halo_widths[:, None]
    return jnp.where(inside[:, None, None, :], filter_values, jnp.zeros_like(filter_values))


def with_neighbours(stacked_rows, upper_row, lower_row, height):
    empty_row = jnp.zeros_like(upper_row)
    joined = jnp.concatenate([upper_row, stacked_rows, empty_row], axis=0)
    return lax.dynamic_update_slice_in_dim(joined, lower_row, height + 1, 0)


def extend_field(values, height):
    last_row = lax.dynamic_slice_in_dim(values, height - 1, 1, 0)
    upper_row = shifted(last_row, "lat", 1)
    lower_row = shifted(values[0:1], "lat", -1)
    joined = with_neighbours(values, upper_row, lower_row, height)
    return padded_2(joined, (("lon", 1),), HALO)


def tile_width(lon_count):
    return max(
        (divisor for divisor in range(1, min(lon_count, 128) + 1) if lon_count % divisor == 0)
    )


def lon_tiles(padded, lon_axis, tile_size):
    lon_count = padded.shape[lon_axis] - 2 * HALO
    pieces = []
    for tile_index in range(lon_count // tile_size):
        begin = tile_index * tile_size
        pieces.append(lax.slice_in_dim(padded, begin, begin + tile_size + 2 * HALO, axis=lon_axis))
    return jnp.stack(pieces, axis=lon_axis)


def band_table(filter_coef, tile_size, reverse):
    span_count = 2 * HALO + 1
    window_rows = jnp.arange(tile_size + 2 * HALO, dtype=jnp.int32)
    window_cols = jnp.arange(tile_size, dtype=jnp.int32)
    distance = window_rows[:, None] - window_cols[None, :]
    if reverse:
        distance = 2 * HALO - distance
    spans = jnp.arange(span_count, dtype=jnp.int32)
    one_hot = (distance[None, :, :] == spans[:, None, None]).astype(jnp.bfloat16)
    band = jnp.einsum("ikab,bpq->ikapq", filter_coef, one_hot, preferred_element_type=jnp.float32)
    return band.astype(jnp.bfloat16)


def apply_filter(padded, filter_coef):
    row_count = filter_coef.shape[0]
    lon_count = padded.shape[1] - 2 * HALO
    tile_size = tile_width(lon_count)
    tiles = lon_tiles(padded, 1, tile_size)
    stacked = jnp.stack([tiles[lat_step : lat_step + row_count] for lat_step in range(3)], axis=1)
    band = band_table(filter_coef, tile_size, False)
    summed = jnp.einsum("iatpc,ikapq->iktqc", stacked, band, preferred_element_type=jnp.float32)
    return summed.reshape((row_count, filter_coef.shape[1], lon_count, padded.shape[2]))


def apply_adjoint(padded, coef_ext):
    row_count = padded.shape[0] - 2
    lon_count = padded.shape[2] - 2 * HALO
    tile_size = tile_width(lon_count)
    tiles = lon_tiles(padded, 2, tile_size)
    band = band_table(coef_ext, tile_size, True)
    tile_count = lon_count // tile_size
    summed = jnp.zeros((row_count, tile_count, tile_size, padded.shape[3]), jnp.float32)
    for lat_step in range(3):
        first_row = 2 - lat_step
        source = tiles[first_row : first_row + row_count]
        weight = band[first_row : first_row + row_count, :, lat_step]
        summed = summed + jnp.einsum(
            "iktpc,ikpq->itqc", source, weight, preferred_element_type=jnp.float32
        )
    return summed.reshape((row_count, lon_count, padded.shape[3]))


def adjoint_field(grad_rows, weights, filter_coef, height):
    last_coef = lax.dynamic_slice_in_dim(filter_coef, height - 1, 1, 0)
    products = jnp.einsum(
        "ijd,kcd->ikjc", grad_rows, weights, preferred_element_type=jnp.float32
    ).astype(jnp.bfloat16)
    last_row = lax.dynamic_slice_in_dim(products, height - 1, 1, 0)
    upper_row, upper_coef = shifted((last_row, last_coef), "lat", 1)
    lower_row, lower_coef = shifted((products[0:1], filter_coef[0:1]), "lat", -1)
    joined = with_neighbours(products, upper_row, lower_row, height)
    padded = padded_2(joined, (("lon", 2),), HALO)
    coef_ext = with_neighbours(filter_coef, upper_coef, lower_coef, height)
    return apply_adjoint(padded, coef_ext)


def layer_total(local_terms):
    return lax.psum(local_terms, ("lat", "lon"))


def per_device(
    state_field, heights, halo_widths, filter_values, weights_one, weights_two, cotangent
):
    height = heights[0]
    slot_count = state_field.shape[0]
    live_mask = (jnp.arange(slot_count, dtype=jnp.int32) < height)[:, None, None]
    filter_coef = masked_filter(filter_values, halo_widths)
    basis_one = apply_filter(extend_field(state_field, height), filter_coef).astype(jnp.bfloat16)
    pre_one = jnp.einsum(
        "ikjc,kcd->ijd", basis_one, weights_one, preferred_element_type=jnp.float32
    )
    hidden = jax.nn.gelu(pre_one, approximate=False).astype(jnp.bfloat16)
    basis_two = apply_filter(extend_field(hidden, height), filter_coef).astype(jnp.bfloat16)
    second_pre = jnp.einsum(
        "ikjc,kcd->ijd", basis_two, weights_two, preferred_element_type=jnp.float32
    )
    next_field = jnp.where(live_mask, second_pre, 0.0).astype(jnp.bfloat16)
    grad_scale = 1.0 / math.sqrt(ROWS * lax.axis_size("lat") * NLON)
    masked_cotangent = jnp.where(live_mask, cotangent, jnp.zeros_like(cotangent))
    local_two = grad_scale * jnp.einsum(
        "ikjc,ijd->kcd", basis_two, masked_cotangent, preferred_element_type=jnp.float32
    )
    grad_weights_two = layer_total(local_two)
    grad_hidden = adjoint_field(masked_cotangent, weights_two, filter_coef, height)
    grad_pre = jnp.where(live_mask, grad_hidden * gelu_slope(pre_one), 0.0).astype(jnp.bfloat16)
    local_one = grad_scale * jnp.einsum(
        "ikjc,ijd->kcd", basis_one, grad_pre, preferred_element_type=jnp.float32
    )
    grad_weights_one = layer_total(local_one)
    grad_input = adjoint_field(grad_pre, weights_one, filter_coef, height)
    grad_field = jnp.where(live_mask, grad_input, 0.0).astype(jnp.bfloat16)
    return (next_field, grad_field, grad_weights_one, grad_weights_two)


def solution(mesh):
    in_specs = (
        P(("groups", "lat"), "lon", None),
        P(("groups", "lat")),
        P(("groups", "lat")),
        P(("groups", "lat"), None, None, None),
        P(),
        P(),
        P(("groups", "lat"), "lon", None),
    )
    out_specs = (
        P(("groups", "lat"), "lon", None),
        P(("groups", "lat"), "lon", None),
        P("groups", None, None),
        P("groups", None, None),
    )
    return jax.shard_map(
        per_device, mesh=mesh, in_specs=in_specs, out_specs=out_specs, check_vma=False
    )
```

profile of v0, /device:TPU:0, one launch (start us, length us, event | category | flops | bytes accessed | tf_op | source)
XLA Modules:
  0.0 306.3 jit_solution(14110254368316311825)
XLA Ops:
  7.9 0.7 broadcast_compare_fusion
  8.7 0.7 broadcast_select_fusion.3
  9.4 1.3 collective-permute-start.9
  10.7 5.5 %collective-permute-start.8 = (bf16[1,3,3,17]{3,0,2,1:T(2,128)(2,1)S(1)}, bf16[1,3,3,17]{3,0,2,1:T(2,128)(2,1)S(1)}, u32[]{:S(2)}, u32[]{:S(2)}) collective-permute-start(bf16[1,3,3,17]{3,0,2,1:T(2,128)(2,1)S(1)} %get-tuple-element.36), channel_id=1, source_target_pairs={{0,2},{2,4},{4,6},{6,8},{8,10},{10,12},{12,14},{1,3},{3,5},{5,7},{... | collective-permute-start | bytes 926 | tf_op jit(solution)/shard_map/ppermute | solution.py:16
  16.2 1.2 fusion.139
  17.3 1.3 collective-permute-start.1
  18.6 5.5 %collective-permute-start = (bf16[1,720,256]{2,1,0:T(8,128)(2,1)S(1)}, bf16[1,720,256]{2,1,0:T(8,128)(2,1)S(1)}, u32[]{:S(2)}, u32[]{:S(2)}) collective-permute-start(bf16[1,720,256]{2,1,0:T(8,128)(2,1)S(1)} %get-tuple-element.34), channel_id=1, source_target_pairs={{0,2},{2,4},{4,6},{6,8},{8,10},{10,12},{12,14},{1,3},{3,5},{5,7},{... | collective-permute-start | bytes 1105928 | tf_op jit(solution)/shard_map/ppermute | solution.py:16
  24.1 2.8 convolution_convert_fusion.1
  27.0 2.1 copy-done.4
  29.0 1.1 dynamic-slice_bitcast_fusion.1
  30.1 5.9 %collective-permute-start.10 = (bf16[1,3,720,256]{3,2,1,0:T(8,128)(2,1)}, bf16[1,3,720,256]{3,2,1,0:T(8,128)(2,1)}, u32[]{:S(2)}, u32[]{:S(2)}) collective-permute-start(bf16[1,3,720,256]{3,2,1,0:T(8,128)(2,1)} %dynamic-slice_bitcast_fusion.1), channel_id=1, source_target_pairs={{0,2},{2,4},{4,6},{6,8},{8,10},{10,12},{12,14},{1,3},{3,5},{5,7},{... | collective-permute-start | bytes 3317768 | tf_op jit(solution)/shard_map/ppermute | solution.py:16
  36.0 1.7 fusion.65
  37.7 2.3 slice.241
  40.1 1.3 collective-permute-start.11
  41.5 0.7 convolution_convert_fusion.2
  42.3 0.3 maximum_maximum_fusion.2
  42.7 0.6 slice_bitcast_fusion.16
  43.2 0.6 collective-permute-start.3
  44.0 0.6 collective-permute-done.3
  44.7 2.1 slice_bitcast_fusion.5
  46.8 38.9 %collective-permute-done.10 = bf16[1,3,720,256]{3,2,1,0:T(8,128)(2,1)} collective-permute-done((bf16[1,3,720,256]{3,2,1,0:T(8,128)(2,1)}, bf16[1,3,720,256]{3,2,1,0:T(8,128)(2,1)}, u32[]{:S(2)}, u32[]{:S(2)}) %collective-permute-start.10) | collective-permute-done | bytes 1105952 | tf_op jit(solution)/shard_map/ppermute | solution.py:16
  85.8 1.9 maximum_maximum_fusion
  87.6 1.3 constant_dynamic-update-slice_fusion.1
  89.1 4.5 %bitcast_convert_fusion.1 = bf16[4,3,120,6,256]{4,2,3,1,0:T(8,128)(2,1)S(1)} fusion(bf16[4,1,6,136,256]{4,3,1,2,0:T(8,128)(2,1)} %get-tuple-element.25, bf16[4,1,6,136,256]{4,3,1,2,0:T(8,128)(2,1)} %get-tuple-element.26, bf16[4,1,6,136,256]{4,3,1,2,0:T(8,128)(2,1)S(1)} %get-tuple-element.24, bf16[4,3,3,136,120,1]{4,0,3,2,1,5:T(4,128)(2,1)S(1)} %copy-done.8), kind=kOutput, calls=%fused_computation.1 | convolution fusion | flops 1822113792 | bytes 10612224 | tf_op jit(solution)/shard_map/iatpc,ikapq->iktqc/dot_general | solution.py:93
  93.6 0.5 collective-permute-start.13
  94.6 0.5 collective-permute-done.13
  95.2 1.5 fusion.133
  96.6 1.2 fusion.13
  97.9 1.2 fusion.15
  99.1 1.3 bitcast_add_fusion.2
  100.4 9.0 %fusion.28 = (bf16[4,720,256]{2,1,0:T(8,128)(2,1)S(1)}, bf16[4,720,256]{2,1,0:T(8,128)(2,1)S(1)}) fusion(f32[4,120,6,256]{3,1,2,0:T(8,128)S(1)} %bitcast_add_fusion.2, pred[4]{0:T(512)(128)(4,1)S(1)} %iota_compare_fusion.2, bf16[4,3,720,256]{3,2,1,0:T(8,128)(2,1)S(1)} %bitcast.339, bf16[3,256,256]{2,1,0:T(8,128)(2,1)S(1)} %copy-done), kind=kOutput, calls=%fused_computation.36 | convolution fusion | flops 1188495360 | bytes 10715140 | tf_op jit(solution)/shard_map/ikjc,kcd->ijd/dot_general | solution.py:141
  109.4 2.3 fusion.77
  111.8 1.3 collective-permute-start.5
  113.1 5.0 %collective-permute-start.4 = (bf16[1,720,256]{2,1,0:T(8,128)(2,1)S(1)}, bf16[1,720,256]{2,1,0:T(8,128)(2,1)S(1)}, u32[]{:S(2)}, u32[]{:S(2)}) collective-permute-start(bf16[1,720,256]{2,1,0:T(8,128)(2,1)S(1)} %get-tuple-element.32), channel_id=1, source_target_pairs={{0,2},{2,4},{4,6},{6,8},{8,10},{10,12},{12,14},{1,3},{3,5},{5,7},{... | collective-permute-start | bytes 1105928 | tf_op jit(solution)/shard_map/ppermute | solution.py:16
  118.2 1.3 convolution_convert_fusion
  119.5 13.8 %collective-permute-done.4 = bf16[1,720,256]{2,1,0:T(8,128)(2,1)S(1)} collective-permute-done((bf16[1,720,256]{2,1,0:T(8,128)(2,1)S(1)}, bf16[1,720,256]{2,1,0:T(8,128)(2,1)S(1)}, u32[]{:S(2)}, u32[]{:S(2)}) %collective-permute-start.4) | collective-permute-done | bytes 368672 | tf_op jit(solution)/shard_map/ppermute | solution.py:16
  133.4 0.3 maximum_maximum_fusion.3
  133.8 1.1 dynamic-slice_bitcast_fusion
  134.8 1.1 slice.253
  135.9 1.3 collective-permute-start.15
  137.2 6.0 %collective-permute-start.14 = (bf16[1,3,720,256]{3,2,1,0:T(8,128)(2,1)}, bf16[1,3,720,256]{3,2,1,0:T(8,128)(2,1)}, u32[]{:S(2)}, u32[]{:S(2)}) collective-permute-start(bf16[1,3,720,256]{3,2,1,0:T(8,128)(2,1)} %dynamic-slice_bitcast_fusion), channel_id=1, source_target_pairs={{0,2},{2,4},{4,6},{6,8},{8,10},{10,12},{12,14},{1,3},{3,5},{5,7},{... | collective-permute-start | bytes 3317768 | tf_op jit(solution)/shard_map/ppermute | solution.py:16
  143.3 0.2 collective-permute-start.7
  143.6 0.8 collective-permute-done.7
  144.5 0.4 slice_bitcast_fusion.2
  144.9 0.9 copy-done.9
  145.8 2.9 bitcast_convert_fusion
  148.7 2.1 copy-done.11
  150.7 2.4 fusion.74
  153.1 36.4 %collective-permute-done.14 = bf16[1,3,720,256]{3,2,1,0:T(8,128)(2,1)} collective-permute-done((bf16[1,3,720,256]{3,2,1,0:T(8,128)(2,1)}, bf16[1,3,720,256]{3,2,1,0:T(8,128)(2,1)}, u32[]{:S(2)}, u32[]{:S(2)}) %collective-permute-start.14) | collective-permute-done | bytes 1105952 | tf_op jit(solution)/shard_map/ppermute | solution.py:16
  189.5 3.2 %maximum_maximum_fusion.1 = bf16[6,3,720,256]{3,2,1,0:T(8,128)(2,1)S(1)} fusion(bf16[4,3,720,256]{3,2,1,0:T(8,128)(2,1)} %bitcast.338, bf16[1,3,720,256]{3,2,1,0:T(8,128)(2,1)} %collective-permute-done.14, bf16[6]{0:T(256)(128)(2,1)S(1)} %pad.36.clone), kind=kLoop, calls=%fused_computation.3 | loop fusion | flops 6635520 | bytes 12165132 | tf_op jit(solution)/shard_map/concatenate | solution.py:46
  192.8 2.8 copy-done.2
  195.6 0.1 collective-permute-start.16
  195.7 2.5 fusion.30
  198.2 0.5 collective-permute-start.17
  198.7 1.6 fusion.87
  200.3 1.1 copy-done.3
  201.9 1.3 fusion.132
  203.2 1.2 fusion.7
  204.4 1.2 fusion.9
  205.7 1.3 bitcast_add_fusion
  207.0 1.5 fusion.29
  208.5 86.8 %all-reduce.3.cloned.1.call-done = (f32[3,256,256]{2,1,0:T(8,128)}, f32[3,256,256]{2,1,0:T(8,128)}) async-done(((f32[3,256,256]{2,1,0:T(8,128)}, f32[3,256,256]{2,1,0:T(8,128)}), (f32[3,256,256]{2,1,0:T(8,128)}, f32[3,256,256]{2,1,0:T(8,128)})) %all-reduce.3.cloned.1.call-update) | async-done | bytes 1572880 | tf_op jit(solution)/shard_map/psum | solution.py:130
  295.3 2.1 copy.145
  297.4 2.1 copy.146
  (82 shorter events, 2.2 us)
Async XLA Ops:
  7.2 93.3 %copy-start = (bf16[3,256,256]{2,1,0:T(8,128)(2,1)S(1)}, bf16[3,256,256]{2,1,0:T(8,128)(2,1)}, u32[]{:S(2)}) copy-start(bf16[3,256,256]{2,1,0:T(8,128)(2,1)} %param.11) | copy-start | bytes 1179652
  7.2 288.1 %all-reduce.3.cloned.1.call-start = ((), (), s32[]{:S(2)}) async-start(), calls=%async_computation | async-start | bytes 3145728 | tf_op jit(solution)/shard_map/psum | solution.py:130
  9.4 32.1 %collective-permute-start.9 = (bf16[1,3,3,17]{3,0,2,1:T(2,128)(2,1)S(1)}, bf16[1,3,3,17]{3,0,2,1:T(2,128)(2,1)S(1)}, u32[]{:S(2)}, u32[]{:S(2)}) collective-permute-start(bf16[1,3,3,17]{3,0,2,1:T(2,128)(2,1)S(1)} %get-tuple-element.35), channel_id=1, source_target_pairs={{2,0},{4,2},{6,4},{8,6},{10,8},{12,10},{14,12},{3,1},{5,3},{7,5},{... | collective-permute-start | bytes 926 | tf_op jit(solution)/shard_map/ppermute | solution.py:16
  10.7 29.4 %collective-permute-start.8 = (bf16[1,3,3,17]{3,0,2,1:T(2,128)(2,1)S(1)}, bf16[1,3,3,17]{3,0,2,1:T(2,128)(2,1)S(1)}, u32[]{:S(2)}, u32[]{:S(2)}) collective-permute-start(bf16[1,3,3,17]{3,0,2,1:T(2,128)(2,1)S(1)} %get-tuple-element.36), channel_id=1, source_target_pairs={{0,2},{2,4},{4,6},{6,8},{8,10},{10,12},{12,14},{1,3},{3,5},{5,7},{... | collective-permute-start | bytes 926 | tf_op jit(solution)/shard_map/ppermute | solution.py:16
  17.3 25.2 %collective-permute-start.1 = (bf16[1,720,256]{2,1,0:T(8,128)(2,1)S(1)}, bf16[1,720,256]{2,1,0:T(8,128)(2,1)S(1)}, u32[]{:S(2)}, u32[]{:S(2)}) collective-permute-start(bf16[1,720,256]{2,1,0:T(8,128)(2,1)S(1)} %get-tuple-element.33), channel_id=1, source_target_pairs={{2,0},{4,2},{6,4},{8,6},{10,8},{12,10},{14,12},{3,1},{5,3},{7,5},{... | collective-permute-start | bytes 1105928 | tf_op jit(solution)/shard_map/ppermute | solution.py:16
  18.6 23.6 %collective-permute-start = (bf16[1,720,256]{2,1,0:T(8,128)(2,1)S(1)}, bf16[1,720,256]{2,1,0:T(8,128)(2,1)S(1)}, u32[]{:S(2)}, u32[]{:S(2)}) collective-permute-start(bf16[1,720,256]{2,1,0:T(8,128)(2,1)S(1)} %get-tuple-element.34), channel_id=1, source_target_pairs={{0,2},{2,4},{4,6},{6,8},{8,10},{10,12},{12,14},{1,3},{3,5},{5,7},{... | collective-permute-start | bytes 1105928 | tf_op jit(solution)/shard_map/ppermute | solution.py:16
  26.9 2.1 copy-start.4
  30.1 55.7 %collective-permute-start.10 = (bf16[1,3,720,256]{3,2,1,0:T(8,128)(2,1)}, bf16[1,3,720,256]{3,2,1,0:T(8,128)(2,1)}, u32[]{:S(2)}, u32[]{:S(2)}) collective-permute-start(bf16[1,3,720,256]{3,2,1,0:T(8,128)(2,1)} %dynamic-slice_bitcast_fusion.1), channel_id=1, source_target_pairs={{0,2},{2,4},{4,6},{6,8},{8,10},{10,12},{12,14},{1,3},{3,5},{5,7},{... | collective-permute-start | bytes 3317768 | tf_op jit(solution)/shard_map/ppermute | solution.py:16
  36.0 6.3 %copy-start.7 = (bf16[4,720,256]{2,1,0:T(8,128)(2,1)S(1)}, bf16[4,720,256]{2,1,0:T(8,128)(2,1)}, u32[]{:S(2)}) copy-start(bf16[4,720,256]{2,1,0:T(8,128)(2,1)} %param.7) | copy-start | bytes 4423684
  40.1 47.5 %collective-permute-start.11 = (bf16[1,3,720,256]{3,2,1,0:T(8,128)(2,1)}, bf16[1,3,720,256]{3,2,1,0:T(8,128)(2,1)}, u32[]{:S(2)}, u32[]{:S(2)}) collective-permute-start(bf16[1,3,720,256]{3,2,1,0:T(8,128)(2,1)} %slice.241), channel_id=1, source_target_pairs={{2,0},{4,2},{6,4},{8,6},{10,8},{12,10},{14,12},{3,1},{5,3},{7,5},{... | collective-permute-start | bytes 3317768 | tf_op jit(solution)/shard_map/ppermute | solution.py:16
  42.6 1.3 collective-permute-start.2
  43.2 1.4 collective-permute-start.3
  44.6 41.1 %slice-start = ((s8[4423680]{0:T(1024)(128)(4,1)}), s8[4194304]{0:T(1024)(128)(4,1)S(1)}, s32[]{:S(2)}) async-start(s8[4423680]{0:T(1024)(128)(4,1)} %bitcast.334), calls=%async_computation.1 | async-start | bytes 8388608
  44.7 41.1 %slice-start.1 = ((s8[4423680]{0:T(1024)(128)(4,1)}), s8[229376]{0:T(1024)(128)(4,1)S(1)}, s32[]{:S(2)}) async-start(s8[4423680]{0:T(1024)(128)(4,1)} %bitcast.334), calls=%async_computation.2 | async-start | bytes 458752
  46.8 42.3 %copy-start.8 = (bf16[4,3,3,136,120,1]{4,0,3,2,1,5:T(4,128)(2,1)S(1)}, bf16[4,3,3,136,120,1]{4,0,3,2,1,5:T(4,128)(2,1)}, u32[]{:S(2)}) copy-start(bf16[4,3,3,136,120,1]{4,0,3,2,1,5:T(4,128)(2,1)} %fusion.65) | copy-start | bytes 3525124
  89.0 5.2 %collective-permute-start.12 = (bf16[6,3,8,256]{3,2,1,0:T(8,128)(2,1)S(1)}, bf16[6,3,8,256]{3,2,1,0:T(8,128)(2,1)S(1)}, u32[]{:S(2)}, u32[]{:S(2)}) collective-permute-start(bf16[6,3,8,256]{3,2,1,0:T(8,128)(2,1)S(1)} %get-tuple-element.15), channel_id=1, source_target_pairs={{0,1},{1,0},{2,3},{3,2},{4,5},{5,4},{6,7},{7,6},{8,9},{9,8},{10,11... | collective-permute-start | bytes 221192 | tf_op jit(solution)/shard_map/ppermute | solution.py:26
  93.6 1.5 collective-permute-start.13
  111.8 21.8 %collective-permute-start.5 = (bf16[1,720,256]{2,1,0:T(8,128)(2,1)S(1)}, bf16[1,720,256]{2,1,0:T(8,128)(2,1)S(1)}, u32[]{:S(2)}, u32[]{:S(2)}) collective-permute-start(bf16[1,720,256]{2,1,0:T(8,128)(2,1)S(1)} %get-tuple-element.31), channel_id=1, source_target_pairs={{2,0},{4,2},{6,4},{8,6},{10,8},{12,10},{14,12},{3,1},{5,3},{7,5},{... | collective-permute-start | bytes 1105928 | tf_op jit(solution)/shard_map/ppermute | solution.py:16
  113.1 20.3 %collective-permute-start.4 = (bf16[1,720,256]{2,1,0:T(8,128)(2,1)S(1)}, bf16[1,720,256]{2,1,0:T(8,128)(2,1)S(1)}, u32[]{:S(2)}, u32[]{:S(2)}) collective-permute-start(bf16[1,720,256]{2,1,0:T(8,128)(2,1)S(1)} %get-tuple-element.32), channel_id=1, source_target_pairs={{0,2},{2,4},{4,6},{6,8},{8,10},{10,12},{12,14},{1,3},{3,5},{5,7},{... | collective-permute-start | bytes 1105928 | tf_op jit(solution)/shard_map/ppermute | solution.py:16
  119.5 15.3 %copy-start.5 = (bf16[4,720,3,256]{3,1,2,0:T(8,128)(2,1)}, bf16[4,720,3,256]{3,1,2,0:T(8,128)(2,1)S(1)}, u32[]{:S(2)}) copy-start(bf16[4,720,3,256]{3,1,2,0:T(8,128)(2,1)S(1)} %convolution_convert_fusion) | copy-start | bytes 13271044
  133.7 9.8 %collective-permute-start.6 = (bf16[6,8,256]{2,1,0:T(8,128)(2,1)S(1)}, bf16[6,8,256]{2,1,0:T(8,128)(2,1)S(1)}, u32[]{:S(2)}, u32[]{:S(2)}) collective-permute-start(bf16[6,8,256]{2,1,0:T(8,128)(2,1)S(1)} %get-tuple-element.28), channel_id=1, source_target_pairs={{0,1},{1,0},{2,3},{3,2},{4,5},{5,4},{6,7},{7,6},{8,9},{9,8},{10,11... | collective-permute-start | bytes 73736 | tf_op jit(solution)/shard_map/ppermute | solution.py:26
  135.9 56.7 %collective-permute-start.15 = (bf16[1,3,720,256]{3,2,1,0:T(8,128)(2,1)}, bf16[1,3,720,256]{3,2,1,0:T(8,128)(2,1)S(1)}, u32[]{:S(2)}, u32[]{:S(2)}) collective-permute-start(bf16[1,3,720,256]{3,2,1,0:T(8,128)(2,1)} %slice.253), channel_id=1, source_target_pairs={{2,0},{4,2},{6,4},{8,6},{10,8},{12,10},{14,12},{3,1},{5,3},{7,5},{... | collective-permute-start | bytes 3317768 | tf_op jit(solution)/shard_map/ppermute | solution.py:16
  137.2 52.3 %collective-permute-start.14 = (bf16[1,3,720,256]{3,2,1,0:T(8,128)(2,1)}, bf16[1,3,720,256]{3,2,1,0:T(8,128)(2,1)}, u32[]{:S(2)}, u32[]{:S(2)}) collective-permute-start(bf16[1,3,720,256]{3,2,1,0:T(8,128)(2,1)} %dynamic-slice_bitcast_fusion), channel_id=1, source_target_pairs={{0,2},{2,4},{4,6},{6,8},{8,10},{10,12},{12,14},{1,3},{3,5},{5,7},{... | collective-permute-start | bytes 3317768 | tf_op jit(solution)/shard_map/ppermute | solution.py:16
  143.3 1.2 collective-permute-start.7
  144.5 1.3 copy-start.9
  145.8 4.9 %copy-start.6 = (bf16[4,720,256]{2,1,0:T(8,128)(2,1)S(1)}, bf16[4,720,256]{2,1,0:T(8,128)(2,1)}, u32[]{:S(2)}) copy-start(bf16[4,720,256]{2,1,0:T(8,128)(2,1)} %param.13) | copy-start | bytes 4423684
  148.7 2.1 copy-start.11
  153.1 42.6 %copy-start.10 = (bf16[3,256,256]{2,1,0:T(8,128)(2,1)S(1)}, bf16[3,256,256]{2,1,0:T(8,128)(2,1)}, u32[]{:S(2)}) copy-start(bf16[3,256,256]{2,1,0:T(8,128)(2,1)} %param.12) | copy-start | bytes 1179652
  153.1 42.6 %copy-start.12 = (bf16[4,3,120,6,256]{4,2,3,1,0:T(8,128)(2,1)S(1)}, bf16[4,3,120,6,256]{4,2,3,1,0:T(8,128)(2,1)}, u32[]{:S(2)}) copy-start(bf16[4,3,120,6,256]{4,2,3,1,0:T(8,128)(2,1)} %copy-done.11) | copy-start | bytes 13271044
  192.8 2.8 copy-start.2
  195.6 3.1 %collective-permute-start.16 = (bf16[6,3,8,256]{3,2,1,0:T(8,128)(2,1)S(1)}, bf16[6,3,8,256]{3,2,1,0:T(8,128)(2,1)S(1)}, u32[]{:S(2)}, u32[]{:S(2)}) collective-permute-start(bf16[6,3,8,256]{3,2,1,0:T(8,128)(2,1)S(1)} %get-tuple-element.13), channel_id=1, source_target_pairs={{0,1},{1,0},{2,3},{3,2},{4,5},{5,4},{6,7},{7,6},{8,9},{9,8},{10,11... | collective-permute-start | bytes 221192 | tf_op jit(solution)/shard_map/ppermute | solution.py:26
  198.2 3.2 %copy-start.3 = (bf16[6,3,720,256]{3,2,1,0:T(8,128)(2,1)S(1)}, bf16[6,3,720,256]{3,2,1,0:T(8,128)(2,1)}, u32[]{:S(2)}) copy-start(bf16[6,3,720,256]{3,2,1,0:T(8,128)(2,1)} %copy-done.2) | copy-start | bytes 19906564
  198.2 3.6 %collective-permute-start.17 = (bf16[6,3,8,256]{3,2,1,0:T(8,128)(2,1)S(1)}, bf16[6,3,8,256]{3,2,1,0:T(8,128)(2,1)S(1)}, u32[]{:S(2)}, u32[]{:S(2)}) collective-permute-start(bf16[6,3,8,256]{3,2,1,0:T(8,128)(2,1)S(1)} %get-tuple-element.12), channel_id=1, source_target_pairs={{1,0},{0,1},{3,2},{2,3},{5,4},{4,5},{7,6},{6,7},{9,8},{8,9},{11,10... | collective-permute-start | bytes 221192 | tf_op jit(solution)/shard_map/ppermute | solution.py:27
  205.6 93.8 %copy-start.1 = (bf16[3,256,256]{2,1,0:T(8,128)(2,1)S(1)}, bf16[3,256,256]{2,1,0:T(8,128)(2,1)}, u32[]{:S(2)}) copy-start(bf16[3,256,256]{2,1,0:T(8,128)(2,1)} %param.11) | copy-start | bytes 1179652
Sparse Core Ops, SparseCore 0:
  198.3 96.9 all-reduce.2
where the time goes:
time: 307 us; the launch traced here: 306 us
  waiting for transfers between devices  178 us (58%)
  matrix products  37.7 us (12%)
  starting transfers between devices  36.6 us (12%)
  local copies, waits for them, and re-layouts  28.2 us (9%)
  between operations  15.3 us (5%)
  other arithmetic  10.5 us (3%)
    ppermute x10, waiting for transfers between devices, shifted(): return lax.ppermute(block, axis, route)  89.2 us
    psum x1, waiting for transfers between devices, layer_total(): return lax.psum(local_terms, ('lat', 'lon'))  86.8 us
    ppermute x10, starting transfers between devices, shifted(): return lax.ppermute(block, axis, route)  34.3 us
    unnamed x48, local copies, waits for them, and re-layouts  14 us
    dot_general x1, matrix products, per_device(): jnp.einsum('ikjc,kcd->ijd', basis_one, weights_one, preferred_element_typ...  8.97 us
    dot_general x6, matrix products, apply_adjoint(): jnp.einsum('iktpc,ikpq->itqc', source, weight, preferred_element_type=jnp...  7.53 us
    dot_general x2, matrix products, apply_filter(): jnp.einsum('iatpc,ikapq->iktqc', stacked, band, preferred_element_type=jn...  7.4 us
  transfers between devices with their start and end apart: 19, of which 7 were waited for; matrix products, arithmetic and copies ran while one was open for 14% of the time, Pallas kernels for 0%

commit v1 on v0

v1 whole, which is shorter than its diff:
```python
import functools
import math

import jax
import jax.numpy as jnp
from jax import lax
from jax.experimental import pallas as pl
from jax.experimental.pallas import tpu as pltpu
from jax.sharding import PartitionSpec as P

NLON = 1440
HALO = 8
ROWS = 2
EDGE = 2 * HALO
TILE = 48
WINDOW = TILE + 2 * EDGE
LANES = 256
CHUNKS = 3
VMEM_LIMIT = 14 * 1024 * 1024
SMALL_LIMIT = 6 * 1024 * 1024


def cost(flops, bytes_accessed):
    return pl.CostEstimate(flops=flops, bytes_accessed=bytes_accessed, transcendentals=0)


def stage_kernel(mode, scale, *refs):
    info_ref, x_ref, ev_ref, od_ref, mix_ref = refs[:5]
    slots, channels = x_ref.shape[0], x_ref.shape[2]
    wide = ev_ref.shape[0] + {"first": 2 * EDGE, "back": -EDGE, "last": 0}[mode]
    lon_count = wide - 2 * EDGE
    height, odd = info_ref[0], info_ref[1]
    own = slice(EDGE, EDGE + lon_count)
    if mode == "first":
        edge_ref, halo_ref, coef_ref, basis_ref, out_ref, slope_ref, ev_out, od_out, band_ref, xe_ref = refs[5:]
    elif mode == "back":
        edge_ref, coef_ref, slope_ref, basis_ref, hidden_ref = refs[5:10]
        out_ref, ext_ref, ev_out, od_out, mine_ref, other_ref = refs[10:16]
        band_ref, terms_ref, xe_ref, acc_one, acc_two = refs[16:]
    else:
        coef_ref, out_ref, band_ref, terms_ref, xe_ref = refs[5:]

    def each_live(act):
        def step(row, carry):
            act(row)
            return carry

        lax.fori_loop(0, height, step, 0)

    def load(row):
        if mode == "last":
            xe_ref[row + 1] = x_ref[row]
        else:
            xe_ref[row + 1, 0:EDGE, :] = edge_ref[row, EDGE : 2 * EDGE, :]
            xe_ref[row + 1, own, :] = x_ref[row]
            xe_ref[row + 1, EDGE + lon_count : wide, :] = edge_ref[row, 0:EDGE, :]

    def load_halo(src_ref, at, slot):
        if mode == "first":
            xe_ref[slot, 0:EDGE, :] = halo_ref[at + EDGE : at + 2 * EDGE, :]
            xe_ref[slot, own, :] = src_ref[...]
            xe_ref[slot, EDGE + lon_count : wide, :] = halo_ref[at : at + EDGE, :]
        else:
            xe_ref[slot] = src_ref[0:wide, :]
        if mode == "back":
            ext_ref[slot] = src_ref[wide : wide + EDGE, :].astype(jnp.float32)[0:8]

    each_live(load)
    if mode == "back":
        ext_ref[1 : slots + 1] = coef_ref[...]
        acc_one[...] = jnp.zeros_like(acc_one)
        acc_two[...] = jnp.zeros_like(acc_two)

    @pl.when(odd == 1)
    def _():
        load_halo(ev_ref, 0, 0)
        load_halo(od_ref, 2 * EDGE, height + 1)

    @pl.when(odd == 0)
    def _():
        load_halo(od_ref, 2 * EDGE, 0)
        load_halo(ev_ref, 0, height + 1)

    zeros_tail = jnp.zeros((LANES - 3 * WINDOW, channels), jnp.bfloat16)
    tiles = lon_count // TILE
    chunk = -(-tiles // CHUNKS)

    def one_row(row):
        rows_ref = ext_ref if mode == "back" else coef_ref
        if rows_ref.shape[0] == slots:
            base = rows_ref[row]
        else:
            lane = lax.broadcasted_iota(jnp.int32, (8, LANES), 1)
            base = jnp.where(
                lane < WINDOW,
                rows_ref[row],
                jnp.where(lane < 2 * WINDOW, rows_ref[row + 1], rows_ref[row + 2]),
            )
        for k in range(3):
            spread = jnp.broadcast_to(base[k : k + 1], (WINDOW, LANES))
            rolled = pltpu.roll(spread, LANES - EDGE, 1, stride=1, stride_axis=0)
            band_ref[row, k * WINDOW : (k + 1) * WINDOW, :] = rolled.astype(jnp.bfloat16)

        def emit(first_tile, last_tile):
            begin, end = EDGE + first_tile * TILE, EDGE + last_tile * TILE
            if mode != "last":
                begin -= EDGE * (first_tile == 0)
                end += EDGE * (last_tile == tiles)
            for tile in range(first_tile, last_tile):
                window = jnp.concatenate(
                    [xe_ref[row + lat_step, tile * TILE : tile * TILE + WINDOW, :] for lat_step in range(3)]
                    + [zeros_tail],
                    axis=0,
                )
                low, high = EDGE, EDGE + TILE
                if mode != "last":
                    low -= EDGE * (tile == 0)
                    high += EDGE * (tile == tiles - 1)
                size = high - low
                band = jnp.concatenate(
                    [band_ref[row, k * WINDOW + low : k * WINDOW + high, :] for k in range(3)], axis=0
                )
                summed = jnp.dot(band, window, preferred_element_type=jnp.float32).astype(jnp.bfloat16)
                for k in range(3):
                    piece = summed[k * size : (k + 1) * size]
                    at = tile * TILE + low
                    span = slice(k * channels, (k + 1) * channels)
                    if mode == "first":
                        basis_ref[row, at : at + size, span] = piece
                    else:
                        terms_ref[at : at + size, span] = piece
            terms = basis_ref[row, begin:end, :] if mode == "first" else terms_ref[begin:end, :]
            mixed = jnp.dot(terms, mix_ref[...], preferred_element_type=jnp.float32)
            if mode == "first":
                cdf = 0.5 * (1.0 + lax.erf(mixed * (1.0 / math.sqrt(2.0))))
                pdf = jnp.exp(-0.5 * mixed * mixed) * (1.0 / math.sqrt(2.0 * math.pi))
                out_ref[row, begin:end, :] = (mixed * cdf).astype(jnp.bfloat16)
                slope_ref[row, begin:end, :] = cdf + mixed * pdf
            elif mode == "back":
                out_ref[row, begin:end, :] = (mixed * slope_ref[row, begin:end, :]).astype(jnp.bfloat16)
            else:
                out_ref[row, begin - EDGE : end - EDGE, :] = mixed.astype(jnp.bfloat16)

        for first_tile in range(0, tiles, chunk):
            emit(first_tile, min(first_tile + chunk, tiles))
        if mode == "back":
            grad_t = out_ref[row, own, :].T
            hidden_t = hidden_ref[row, own, :].T
            for k in range(3):
                span = slice(k * channels, (k + 1) * channels)
                acc_one[:, span] += jnp.dot(grad_t, basis_ref[row, own, span], preferred_element_type=jnp.float32)
                acc_two[:, span] += jnp.dot(hidden_t, terms_ref[own, span], preferred_element_type=jnp.float32)

    each_live(one_row)
    if mode == "last":

        def clear(row, carry):
            out_ref[row] = jnp.zeros(out_ref.shape[1:], out_ref.dtype)
            return carry

        lax.fori_loop(height, slots, clear, 0)
    else:
        ev_out[...] = out_ref[info_ref[2]]
        od_out[...] = out_ref[info_ref[3]]
        if mode == "back":

            def write(one_ref, two_ref):
                for k in range(3):
                    span = slice(k * channels, (k + 1) * channels)
                    one_ref[span] = (acc_one[:, span].T * scale).astype(one_ref.dtype)
                    two_ref[span] = (acc_two[:, span] * scale).astype(two_ref.dtype)

            @pl.when(info_ref[4] == 0)
            def _():
                write(mine_ref, other_ref)

            @pl.when(info_ref[4] != 0)
            def _():
                write(other_ref, mine_ref)


def stage(mode, estimate, info, x, ev, od, mix, *extra, scale=None):
    slots, channels = x.shape[0], x.shape[2]
    wide = ev.shape[0] + {"first": 2 * EDGE, "back": -EDGE, "last": 0}[mode]
    lon_count = wide - 2 * EDGE
    bf16, f32 = jnp.bfloat16, jnp.float32
    vmem = pl.BlockSpec(memory_space=pltpu.VMEM)
    basis = ((slots, wide, 3 * channels), bf16)
    field = ((slots, wide, channels), bf16)
    slope = ((slots, wide, channels), f32)
    band = ((slots, 3 * WINDOW, LANES), bf16)
    row = ((wide, channels), bf16)
    terms = ((wide, 3 * channels), bf16)
    ext = ((slots + 2, wide, channels), bf16)
    sums = (3 * channels, channels)
    if mode == "first":
        outs = (basis, field, slope, row, row)
        scratch = [band, ext]
    elif mode == "back":
        outs = (field, ((slots + 2, 8, LANES), f32), row, row, (sums, f32), (sums, bf16))
        acc = ((channels, 3 * channels), f32)
        scratch = [band, terms, ext, acc, acc]
    else:
        outs = (((slots, lon_count, channels), bf16),)
        scratch = [band, terms, ext]
    return pl.pallas_call(
        functools.partial(stage_kernel, mode, scale),
        out_shape=tuple(jax.ShapeDtypeStruct(*array) for array in outs),
        in_specs=[pl.BlockSpec(memory_space=pltpu.SMEM)] + [vmem] * (4 + len(extra)),
        out_specs=(vmem,) * len(outs),
        scratch_shapes=[pltpu.VMEM(*array) for array in scratch],
        compiler_params=pltpu.CompilerParams(vmem_limit_bytes=VMEM_LIMIT),
        cost_estimate=estimate,
    )(info, x, ev, od, mix, *extra)


def pack_kernel(which, info_ref, x_ref, edge_ref, tile_ref, out_ref, sem):
    lon_count = x_ref.shape[1]
    wide = lon_count + 2 * EDGE
    row = info_ref[which]
    copy = pltpu.make_async_copy(x_ref.at[row], out_ref.at[EDGE : EDGE + lon_count], sem)
    copy.start()
    out_ref[0:EDGE] = edge_ref[row, EDGE : 2 * EDGE]
    out_ref[EDGE + lon_count : wide] = edge_ref[row, 0:EDGE]
    out_ref[wide : wide + EDGE] = tile_ref[row]
    copy.wait()


def pack(which, info, x, edges, tiles, after=()):
    row = jax.ShapeDtypeStruct((x.shape[1] + 3 * EDGE, x.shape[2]), x.dtype)
    kernel = functools.partial(pack_kernel, which)
    (out,) = local_call(
        kernel, info, (row,), SMALL_LIMIT, cost(0, 4 * row.size), (edges, tiles), (pltpu.SemaphoreType.DMA,), (x,), after
    )
    return out


def local_call(kernel, info, outs, limit, estimate, operands, scratch=(), far=(), after=()):
    vmem, anywhere = pl.BlockSpec(memory_space=pltpu.VMEM), pl.BlockSpec(memory_space=pl.ANY)

    def body(info_ref, *refs):
        kernel(info_ref, *refs[len(after) :])

    return pl.pallas_call(
        body,
        out_shape=tuple(outs),
        in_specs=[pl.BlockSpec(memory_space=pltpu.SMEM)]
        + [anywhere] * (len(after) + len(far))
        + [vmem] * len(operands),
        out_specs=(vmem,) * len(outs),
        scratch_shapes=list(scratch),
        compiler_params=pltpu.CompilerParams(vmem_limit_bytes=limit),
        cost_estimate=estimate,
    )(info, *after, *far, *operands)


def pass_kernel(info_ref, value_ref, out_ref):
    out_ref[...] = value_ref[...]


def pass_after(info, value, after):
    (out,) = local_call(pass_kernel, info, (jax.ShapeDtypeStruct(value.shape, value.dtype),), SMALL_LIMIT, cost(1, 1), (value,), after=after)
    return out


def sum_kernel(info_ref, *refs):
    total = refs[0][...].astype(jnp.float32)
    for ref in refs[1:-1]:
        total += ref[...].astype(jnp.float32)
    refs[-1][...] = total.astype(jnp.bfloat16)


def rounded_sum(info, terms, after):
    out = jax.ShapeDtypeStruct(terms[0].shape, jnp.bfloat16)
    return local_call(sum_kernel, info, (out,), SMALL_LIMIT, cost(1, 1), terms, after=after)[0]


def split_kernel(info_ref, mine_ref, heard_ref, own_ref, *send_refs):
    rows = own_ref.shape[0]
    for step in range(4):
        at = pl.ds(pl.multiple_of((info_ref[5] ^ step) * rows, rows), rows)
        piece = mine_ref[at, :] + heard_ref[at, :].astype(jnp.float32)
        if step == 0:
            own_ref[...] = piece
        else:
            send_refs[step - 1][...] = piece.astype(jnp.bfloat16)


def join_kernel(info_ref, *refs):
    first_ref, second_ref = refs[8:]
    rows = refs[0].shape[0]

    def write(mine_ref, other_ref):
        for step in range(4):
            at = pl.ds(pl.multiple_of((info_ref[5] ^ step) * rows, rows), rows)
            mine_ref[at, :] = refs[step][...].astype(jnp.float32)
            other_ref[at, :] = refs[4 + step][...].astype(jnp.float32)

    @pl.when(info_ref[4] == 0)
    def _():
        write(first_ref, second_ref)

    @pl.when(info_ref[4] != 0)
    def _():
        write(second_ref, first_ref)


def coef_lanes(coef):
    slots, basis_count, steps, spans = coef.shape
    wide = jnp.pad(coef, ((0, 0), (0, 0), (0, 0), (HALO, WINDOW - HALO - spans)))
    wide = wide.reshape(slots, basis_count, steps * WINDOW)
    return jnp.pad(wide, ((0, 0), (0, 8 - basis_count), (0, LANES - steps * WINDOW)))


def edge_columns(x):
    lon_count = x.shape[-2]
    return jnp.concatenate([x[..., :EDGE, :], x[..., lon_count - EDGE :, :]], axis=-2)


def ev_swap(row):
    return lax.ppermute(row, "lat", [(i, i ^ 1) for i in range(lax.axis_size("lat"))])


def od_swap(row):
    return lax.ppermute(row, "lat", [(i, i + 1 if i % 2 else i - 1) for i in range(1, lax.axis_size("lat") - 1)])


def row_swap(ev, od):
    return ev_swap(ev), od_swap(od)


def partner(value):
    return lax.ppermute(value, "lon", [(0, 1), (1, 0)])


def across(value, step):
    size = lax.axis_size("lat")
    low = size // 4
    return lax.ppermute(value, "lat", [(i, ((i // low) ^ step) * low + i % low) for i in range(size)])


def cut_terms(info, mine, other):
    piece = jax.ShapeDtypeStruct((mine.shape[0] // 4, mine.shape[1]), jnp.bfloat16)
    outs = (jax.ShapeDtypeStruct(piece.shape, jnp.float32), piece, piece, piece)
    own, *sends = local_call(split_kernel, info, outs, SMALL_LIMIT, cost(1, 1), (mine, partner(other)))
    return own, sends


def total(info, own, sends, before_swap, before_gather, before_join):
    size = lax.axis_size("lat")
    held = rounded_sum(info, [own] + [across(sends[step - 1], step) for step in (1, 2, 3)], before_swap)
    stride = 1
    while stride < size // 4:
        heard = lax.ppermute(held, "lat", [(i, i ^ stride) for i in range(size)])
        stride *= 2
        held = rounded_sum(info, [held, heard], before_gather if stride == size // 4 else ())
    pieces = [held] + [across(held, step) for step in (1, 2, 3)]
    pieces, _ = lax.optimization_barrier((pieces, before_join))
    pieces += [partner(value) for value in pieces]
    whole = jax.ShapeDtypeStruct((4 * held.shape[0], held.shape[1]), jnp.float32)
    return local_call(join_kernel, info, (whole, whole), SMALL_LIMIT, cost(1, 1), pieces)


def per_device(state_field, heights, halo_widths, filter_values, weights_one, weights_two, cotangent):
    height = heights[0]
    spans = filter_values.shape[-1]
    channels = state_field.shape[2]
    place = lax.axis_index("lat")
    odd = lax.rem(place, 2)
    last = height - 1
    ev_row, od_row = jnp.where(odd == 1, 0, last), jnp.where(odd == 1, last, 0)

    ev = lax.dynamic_index_in_dim(state_field, ev_row, 0, keepdims=False)
    od = lax.dynamic_index_in_dim(state_field, od_row, 0, keepdims=False)
    state_ev, state_od = row_swap(ev, od)
    state_field, cotangent, halo_widths, ev, od = lax.optimization_barrier((state_field, cotangent, halo_widths, ev, od))

    info = jnp.stack([height, odd, ev_row, od_row, lax.axis_index("lon"), place // (lax.axis_size("lat") // 4)])
    info = info.astype(jnp.int32)
    offsets = jnp.abs(jnp.arange(spans, dtype=jnp.int32) - (spans - 1) // 2)
    inside = offsets[None, :] <= halo_widths[:, None]
    coef = jnp.where(inside[:, None, None, :], filter_values, jnp.zeros_like(filter_values))
    forward = coef_lanes(coef).astype(jnp.float32)
    backward = coef_lanes(coef[:, :, ::-1, ::-1])
    backward_tile = jnp.pad(backward, ((0, 0), (0, EDGE - 8), (0, 0)))
    mix_one = weights_one.reshape(3 * channels, channels)
    mix_two = weights_two.reshape(3 * channels, channels)
    mix_one_t = jnp.swapaxes(weights_one, 1, 2).reshape(3 * channels, channels)
    mix_two_t = jnp.swapaxes(weights_two, 1, 2).reshape(3 * channels, channels)

    edges_s = partner(edge_columns(state_field))
    edges_c = partner(edge_columns(cotangent))
    cot_ev = ev_swap(pack(2, info, cotangent, edges_c, backward_tile))
    cot_od = od_swap(pack(3, info, cotangent, edges_c, backward_tile, (state_ev, state_od)))
    halo_edges = partner(jnp.concatenate([edge_columns(state_ev), edge_columns(state_od)], axis=0))

    points = state_field.shape[0] * state_field.shape[1]
    flops = 2 * points * channels * (9 * WINDOW + 3 * channels)
    full, most = cost(flops, points * channels * 16), cost(3 * flops, points * channels * 24)
    basis_one, hidden, slope, ev, od = stage(
        "first", full, info, state_field, state_ev, state_od, mix_one, edges_s, halo_edges, forward
    )
    hidden_ev, hidden_od = row_swap(ev, od)
    scale = 1.0 / math.sqrt(ROWS * lax.axis_size("lat") * NLON)
    grad_pre, backward_ext, ev, od, mine, other = stage(
        "back", most, info, cotangent, cot_ev, cot_od, mix_two_t, edges_c, backward.astype(jnp.float32),
        slope, basis_one, hidden, scale=scale,
    )
    other = pass_after(info, other, (hidden_ev, hidden_od))
    own, sends = cut_terms(info, mine, other)
    grad_ev, grad_od = row_swap(ev, od)
    (next_field,) = stage("last", full, info, hidden, hidden_ev, hidden_od, mix_two, forward)
    (grad_field,) = stage("last", full, info, grad_pre, grad_ev, grad_od, mix_one_t, backward_ext)
    grad_one, grad_two = total(info, own, sends, (next_field,), (grad_ev, grad_od), grad_field)
    return next_field, grad_field, grad_one.reshape(weights_one.shape), grad_two.reshape(weights_two.shape)


def solution(mesh):
    in_specs = (
        P(("groups", "lat"), "lon", None),
        P(("groups", "lat")),
        P(("groups", "lat")),
        P(("groups", "lat"), None, None, None),
        P(),
        P(),
        P(("groups", "lat"), "lon", None),
    )
    out_specs = (
        P(("groups", "lat"), "lon", None),
        P(("groups", "lat"), "lon", None),
        P("groups", None, None),
        P("groups", None, None),
    )
    return jax.shard_map(
        per_device, mesh=mesh, in_specs=in_specs, out_specs=out_specs, check_vma=False
    )
```

time: 307 us -> 103 us (0.34)
  waiting for transfers between devices: 178 us -> 37.4 us
  matrix products: 37.7 us -> 0 us
  Pallas kernels: 0 us -> 19.3 us
  local copies, waits for them, and re-layouts: 28.2 us -> 10.6 us
  between operations: 15.3 us -> 1.65 us
  other arithmetic: 10.5 us -> 1.35 us
  starting transfers between devices: 36.6 us -> 32.9 us
    psum x1 -> x0, waiting for transfers between devices: 86.8 us -> none  [layer_total(): return lax.psum(local_terms, ('lat', 'lon'))]
    ppermute x18 -> x23, waiting for transfers between devices: 91.1 us -> 37.4 us  [the longest x4 20.6 us: ev_swap(): lax.ppermute(row, 'lat', [(i, i ^ 1) for i in range(lax.axis_size('lat'))])]
    dot_general x16 -> x0, matrix products: 37.7 us -> none  [the longest x1 8.97 us: per_device(): jnp.einsum('ikjc,kcd->ijd', basis_one, weights_one, preferred_element_typ...]
    pallas_call x0 -> x11, Pallas kernels: none -> 19.3 us  [the longest x4 12.2 us: stage(): pl.pallas_call(functools.partial(stage_kernel, mode, scale), out_shape=tu...]
    unnamed x48 -> x26, local copies, waits for them, and re-layouts: 14 us -> 3.81 us
    slice x11 -> x4, local copies, waits for them, and re-layouts: 7.42 us -> 1.5 us  [edge_columns(): x[..., :EDGE, :]]
    concatenate x5 -> x3, other arithmetic: 5.64 us -> 1.24 us  [the longest x2 0.64 us: edge_columns(): jnp.concatenate([x[..., :EDGE, :], x[..., lon_count - EDGE:, :]], axis=-2)]
    ppermute x18 -> x23, starting transfers between devices: 36.5 us -> 32.9 us  [the longest x4 17.4 us: ev_swap(): lax.ppermute(row, 'lat', [(i, i ^ 1) for i in range(lax.axis_size('lat'))])]
  transfers between devices with their start and end apart: 19 -> 23, of which waited for: 7 -> 12; matrix products, arithmetic and copies ran while one was open for 14% -> 6% of each run, Pallas kernels for 0% -> 16%
where the time goes in v1:
time: 103 us
  waiting for transfers between devices  37.4 us (36%)
  starting transfers between devices  32.9 us (32%)
  Pallas kernels  19.3 us (19%)
  local copies, waits for them, and re-layouts  10.6 us (10%)
  between operations  1.65 us (2%)
  other arithmetic  1.35 us (1%)
    ppermute x4, waiting for transfers between devices, ev_swap(): lax.ppermute(row, 'lat', [(i, i ^ 1) for i in range(lax.axis_size('lat'))])  20.6 us
    ppermute x4, starting transfers between devices, ev_swap(): lax.ppermute(row, 'lat', [(i, i ^ 1) for i in range(lax.axis_size('lat'))])  17.4 us
    pallas_call x4, Pallas kernels, stage(): pl.pallas_call(functools.partial(stage_kernel, mode, scale), out_shape=tu...  12.2 us
    ppermute x6, waiting for transfers between devices, across(): lax.ppermute(value, 'lat', [(i, (i // low ^ step) * low + i % low) for i...  11.4 us
    ppermute x6, starting transfers between devices, across(): lax.ppermute(value, 'lat', [(i, (i // low ^ step) * low + i % low) for i...  9.66 us
    pallas_call x7, Pallas kernels, local_call(): pl.pallas_call(body, out_shape=tuple(outs), in_specs=[pl.BlockSpec(memory...  7.08 us
    ppermute x1, waiting for transfers between devices, total(): heard = lax.ppermute(held, 'lat', [(i, i ^ stride) for i in range(size)])  4.4 us
    ppermute x4, starting transfers between devices, od_swap(): lax.ppermute(row, 'lat', [(i, i + 1 if i % 2 else i - 1) for i in range(1...  4.19 us
  transfers between devices with their start and end apart: 23, of which 12 were waited for; matrix products, arithmetic and copies ran while one was open for 6% of the time, Pallas kernels for 16%

profile of v1, /device:TPU:0, one launch (start us, length us, event | category | flops | bytes accessed | tf_op | source)
XLA Modules:
  0.0 103.2 jit_solution(7655027448005398448)
XLA Ops:
  1.4 2.0 %dynamic-slice_bitcast_fusion = (bf16[720,256]{1,0:T(8,128)(2,1)}, bf16[720,256]{1,0:T(8,128)(2,1)}) fusion(bf16[4,720,256]{2,1,0:T(8,128)(2,1)} %refs_1_, s32[]{:T(128)S(6)} %select_n.28, s32[]{:T(128)S(6)} %select_n.27), kind=kLoop, calls=%fused_computation | loop fusion | bytes 1474568 | tf_op jit(solution)/shard_map/jit(dynamic_index_in_dim)/squeeze | solution.py:374
  3.5 3.0 %collective-permute-start = (bf16[720,256]{1,0:T(8,128)(2,1)}, bf16[720,256]{1,0:T(8,128)(2,1)S(1)}, u32[]{:S(2)}, u32[]{:S(2)}) collective-permute-start(bf16[720,256]{1,0:T(8,128)(2,1)} %get-tuple-element.57), channel_id=1, source_target_pairs={{0,2},{2,0},{4,6},{6,4},{8,10},{10,8},{12,14},{14,12},{1,3},{3,1},... | collective-permute-start | bytes 1105928 | tf_op jit(solution)/shard_map/ppermute | solution.py:321
  6.4 1.4 %collective-permute-start.1 = (bf16[720,256]{1,0:T(8,128)(2,1)}, bf16[720,256]{1,0:T(8,128)(2,1)}, u32[]{:S(2)}, u32[]{:S(2)}) collective-permute-start(bf16[720,256]{1,0:T(8,128)(2,1)} %get-tuple-element.56), channel_id=1, source_target_pairs={{2,4},{4,2},{6,8},{8,6},{10,12},{12,10},{3,5},{5,3},{7,9},{9,7},{1... | collective-permute-start | bytes 1105928 | tf_op jit(solution)/shard_map/ppermute | solution.py:325
  7.8 0.8 fusion.1
  8.6 0.6 pad_maximum_fusion
  9.3 0.6 collective-permute-start.6
  9.8 0.1 broadcast_compare_fusion
  9.9 0.1 rev.3
  10.0 0.1 pad.18.clone
  10.1 0.7 reshape.70
  10.8 0.1 pad.20.clone
  10.9 0.1 reshape.71
  11.0 0.1 stack.23.refs_0_.info_ref
  11.1 1.5 %shard_map.104 = bf16[768,256]{1,0:T(8,128)(2,1)} custom-call(s32[6]{0:T(128)S(1)} %stack.23.refs_0_.info_ref, bf16[4,720,256]{2,1,0:T(8,128)(2,1)S(1)} %copy-done, bf16[4,32,256]{2,1,0:T(8,128)(2,1)S(1)} %collective-permute-done.6.refs_1_.refs_3_.refs_5_, bf16[4,16,256]{2,1,0:T(8,128)(2,1)S(1)} %pad.22.refs_2_.refs_4_), custom_call_target="tpu_custom_call" | custom-call | bytes 786432 | tf_op jit(solution)/shard_map/pallas_call | solution.py:244
  12.6 0.0 copy-start.2
  12.6 3.6 %collective-permute-start.7 = (bf16[768,256]{1,0:T(8,128)(2,1)}, bf16[768,256]{1,0:T(8,128)(2,1)}, u32[]{:S(2)}, u32[]{:S(2)}) collective-permute-start(bf16[768,256]{1,0:T(8,128)(2,1)} %shard_map.104), channel_id=1, source_target_pairs={{0,2},{2,0},{4,6},{6,4},{8,10},{10,8},{12,14},{14,12},{1,3},{3,1},... | collective-permute-start | bytes 1179656 | tf_op jit(solution)/shard_map/ppermute | solution.py:321
  16.2 7.4 %collective-permute-done.refs_2_.refs_0_ = bf16[720,256]{1,0:T(8,128)(2,1)S(1)} collective-permute-done((bf16[720,256]{1,0:T(8,128)(2,1)}, bf16[720,256]{1,0:T(8,128)(2,1)S(1)}, u32[]{:S(2)}, u32[]{:S(2)}) %collective-permute-start) | collective-permute-done | bytes 368672 | tf_op jit(solution)/shard_map/ppermute | solution.py:321
  23.6 1.5 %shard_map.105 = bf16[768,256]{1,0:T(8,128)(2,1)} custom-call(s32[6]{0:T(128)S(1)} %stack.23.refs_0_.info_ref, bf16[720,256]{1,0:T(8,128)(2,1)S(1)} %collective-permute-done.refs_2_.refs_0_, bf16[720,256]{1,0:T(8,128)(2,1)} %collective-permute-done.1.refs_3_.refs_1_, bf16[4,720,256]{2,1,0:T(8,128)(2,1)S(1)} %copy-done, ...), custom_call_target="tpu_custom_call" | custom-call | bytes 786432 | tf_op jit(solution)/shard_map/pallas_call | solution.py:244
  25.1 1.4 %collective-permute-start.8 = (bf16[768,256]{1,0:T(8,128)(2,1)}, bf16[768,256]{1,0:T(8,128)(2,1)}, u32[]{:S(2)}, u32[]{:S(2)}) collective-permute-start(bf16[768,256]{1,0:T(8,128)(2,1)} %shard_map.105), channel_id=1, source_target_pairs={{2,4},{4,2},{6,8},{8,6},{10,12},{12,10},{3,5},{5,3},{7,9},{9,7},{1... | collective-permute-start | bytes 1179656 | tf_op jit(solution)/shard_map/ppermute | solution.py:325
  26.5 0.7 fusion.3
  27.3 0.6 pad_maximum_fusion.2
  27.9 0.0 collective-permute-start.3
  27.9 1.9 %copy.19 = bf16[3,256,256]{2,1,0:T(8,128)(2,1)} copy(bf16[3,256,256]{1,2,0:T(8,128)(2,1)} %bitcast.18) | data formatting | bytes 786432 | tf_op jit(solution)/shard_map/transpose | solution.py:389
  29.8 0.0 collective-permute-done.2.refs_5_
  29.8 0.0 copy-start.4
  29.8 1.0 copy-done.4
  30.8 2.3 %shard_map.102 = (bf16[4,752,768]{2,1,0:T(8,128)(2,1)S(1)}, bf16[4,752,256]{2,1,0:T(8,128)(2,1)S(1)}, f32[4,752,256]{2,1,0:T(8,128)S(1)}, bf16[752,256]{1,0:T(8,128)(2,1)S(1)}, bf16[752,256]{1,0:T(8,128)(2,1)S(1)}) custom-call(s32[6]{0:T(128)S(1)} %stack.23.refs_0_.info_ref, bf16[4,720,256]{2,1,0:T(8,128)(2,1)S(1)} %copy-done.2, ...), custom_call_target="tpu_custom_call" | custom-call | flops 2194145280 | bytes 11796480 | tf_op jit(solution)/shard_map/pallas_call | solution.py:206
  33.1 4.5 %collective-permute-start.4 = (bf16[752,256]{1,0:T(8,128)(2,1)S(1)}, bf16[752,256]{1,0:T(8,128)(2,1)S(1)}, u32[]{:S(2)}, u32[]{:S(2)}) collective-permute-start(bf16[752,256]{1,0:T(8,128)(2,1)S(1)} %get-tuple-element.31), channel_id=1, source_target_pairs={{0,2},{2,0},{4,6},{6,4},{8,10},{10,8},{12,14},{14,12},{1,3},{3,1},... | collective-permute-start | bytes 1155080 | tf_op jit(solution)/shard_map/ppermute | solution.py:321
  37.5 0.7 collective-permute-start.5
  38.2 2.1 %collective-permute-done.7.refs_2_ = bf16[768,256]{1,0:T(8,128)(2,1)} collective-permute-done((bf16[768,256]{1,0:T(8,128)(2,1)}, bf16[768,256]{1,0:T(8,128)(2,1)}, u32[]{:S(2)}, u32[]{:S(2)}) %collective-permute-start.7) | collective-permute-done | bytes 393248 | tf_op jit(solution)/shard_map/ppermute | solution.py:321
  40.4 0.0 collective-permute-done.8.refs_3_
  40.4 4.3 %shard_map.106 = (bf16[4,752,256]{2,1,0:T(8,128)(2,1)S(1)}, f32[6,8,256]{2,1,0:T(8,128)S(1)}, bf16[752,256]{1,0:T(8,128)(2,1)}, bf16[752,256]{1,0:T(8,128)(2,1)}...) custom-call(s32[6]{0:T(128)S(1)} %stack.23.refs_0_.info_ref, bf16[4,720,256]{2,1,0:T(8,128)(2,1)S(1)} %copy-done, ...), custom_call_target="tpu_custom_call" | custom-call | flops 6582435840 | bytes 17694720 | tf_op jit(solution)/shard_map/pallas_call | solution.py:206
  44.6 11.1 %collective-permute-done.4.refs_2_.refs_0_ = bf16[752,256]{1,0:T(8,128)(2,1)S(1)} collective-permute-done((bf16[752,256]{1,0:T(8,128)(2,1)S(1)}, bf16[752,256]{1,0:T(8,128)(2,1)S(1)}, u32[]{:S(2)}, u32[]{:S(2)}) %collective-permute-start.4) | collective-permute-done | bytes 385056 | tf_op jit(solution)/shard_map/ppermute | solution.py:321
  55.7 0.6 shard_map.108
  56.3 0.1 collective-permute-start.11
  56.4 0.7 collective-permute-start.10
  57.1 6.3 %collective-permute-start.9 = (bf16[752,256]{1,0:T(8,128)(2,1)}, bf16[752,256]{1,0:T(8,128)(2,1)S(1)}, u32[]{:S(2)}, u32[]{:S(2)}) collective-permute-start(bf16[752,256]{1,0:T(8,128)(2,1)} %get-tuple-element.37), channel_id=1, source_target_pairs={{0,2},{2,0},{4,6},{6,4},{8,10},{10,8},{12,14},{14,12},{1,3},{3,1},... | collective-permute-start | bytes 1155080 | tf_op jit(solution)/shard_map/ppermute | solution.py:321
  63.4 0.6 shard_map.109
  64.0 2.8 %collective-permute-start.12 = (bf16[192,256]{1,0:T(8,128)(2,1)S(1)}, bf16[192,256]{1,0:T(8,128)(2,1)S(1)}, u32[]{:S(2)}, u32[]{:S(2)}) collective-permute-start(bf16[192,256]{1,0:T(8,128)(2,1)S(1)} %get-tuple-element.43), channel_id=1, source_target_pairs={{0,4},{2,6},{4,0},{6,2},{8,12},{10,14},{12,8},{14,10},{1,5},{3,7},... | collective-permute-start | bytes 294920 | tf_op jit(solution)/shard_map/ppermute | solution.py:339
  66.8 2.4 %collective-permute-start.14 = (bf16[192,256]{1,0:T(8,128)(2,1)S(1)}, bf16[192,256]{1,0:T(8,128)(2,1)S(1)}, u32[]{:S(2)}, u32[]{:S(2)}) collective-permute-start(bf16[192,256]{1,0:T(8,128)(2,1)S(1)} %get-tuple-element.45), channel_id=1, source_target_pairs={{0,12},{2,14},{4,8},{6,10},{8,4},{10,6},{12,0},{14,2},{1,13},{3,15... | collective-permute-start | bytes 294920 | tf_op jit(solution)/shard_map/ppermute | solution.py:339
  69.3 2.8 %shard_map.103.refs_0_ = bf16[4,720,256]{2,1,0:T(8,128)(2,1)} custom-call(s32[6]{0:T(128)S(1)} %stack.23.refs_0_.info_ref, bf16[4,752,256]{2,1,0:T(8,128)(2,1)S(1)} %get-tuple-element.30.refs_1_.refs_9_, bf16[752,256]{1,0:T(8,128)(2,1)S(1)} %collective-permute-done.4.refs_2_.refs_0_, bf16[752,256]{1,0:T(8,128)(2,1)S(1)} %collective-permute-done.5.refs_3_.refs_1_, ...), custom_call_target="tpu_custom_call" | custom-call | flops 2194145280 | bytes 11796480 | tf_op jit(solution)/shard_map/pallas_call | solution.py:206
  72.1 2.0 %collective-permute-done.12.refs_2_ = bf16[192,256]{1,0:T(8,128)(2,1)S(1)} collective-permute-done((bf16[192,256]{1,0:T(8,128)(2,1)S(1)}, bf16[192,256]{1,0:T(8,128)(2,1)S(1)}, u32[]{:S(2)}, u32[]{:S(2)}) %collective-permute-start.12) | collective-permute-done | bytes 98336 | tf_op jit(solution)/shard_map/ppermute | solution.py:339
  74.1 2.0 %collective-permute-done.13.refs_3_ = bf16[192,256]{1,0:T(8,128)(2,1)S(1)} collective-permute-done((bf16[192,256]{1,0:T(8,128)(2,1)S(1)}, bf16[192,256]{1,0:T(8,128)(2,1)S(1)}, u32[]{:S(2)}, u32[]{:S(2)}) %collective-permute-start.13) | collective-permute-done | bytes 98336 | tf_op jit(solution)/shard_map/ppermute | solution.py:339
  76.1 5.0 %collective-permute-done.14.refs_4_ = bf16[192,256]{1,0:T(8,128)(2,1)S(1)} collective-permute-done((bf16[192,256]{1,0:T(8,128)(2,1)S(1)}, bf16[192,256]{1,0:T(8,128)(2,1)S(1)}, u32[]{:S(2)}, u32[]{:S(2)}) %collective-permute-start.14) | collective-permute-done | bytes 98336 | tf_op jit(solution)/shard_map/ppermute | solution.py:339
  81.1 1.4 %copy-done.1 = bf16[4,720,256]{2,1,0:T(8,128)(2,1)S(1)} copy-done((bf16[4,720,256]{2,1,0:T(8,128)(2,1)S(1)}, bf16[4,720,256]{2,1,0:T(8,128)(2,1)}, u32[]{:S(2)}) %copy-start.1) | copy-done | bytes 1474584
  82.5 0.6 shard_map.110.refs_2_
  83.1 0.1 collective-permute-start.15
  83.2 0.2 copy.20
  83.4 4.4 %collective-permute-done.15.refs_3_ = bf16[192,256]{1,0:T(8,128)(2,1)S(1)} collective-permute-done((bf16[192,256]{1,0:T(8,128)(2,1)S(1)}, bf16[192,256]{1,0:T(8,128)(2,1)S(1)}, u32[]{:S(2)}, u32[]{:S(2)}) %collective-permute-start.15) | collective-permute-done | bytes 98336 | tf_op jit(solution)/shard_map/ppermute | solution.py:354
  87.8 0.6 shard_map.111.refs_0_
  88.4 1.7 %collective-permute-start.16 = (bf16[192,256]{1,0:T(8,128)(2,1)S(1)}, bf16[192,256]{1,0:T(8,128)(2,1)S(1)}, u32[]{:S(2)}, u32[]{:S(2)}) collective-permute-start(bf16[192,256]{1,0:T(8,128)(2,1)S(1)} %shard_map.111.refs_0_), channel_id=1, source_target_pairs={{0,4},{2,6},{4,0},{6,2},{8,12},{10,14},{12,8},{14,10},{1,5},{3,7},... | collective-permute-start | bytes 294920 | tf_op jit(solution)/shard_map/ppermute | solution.py:339
  90.1 0.8 collective-permute-start.17
  90.9 2.0 %collective-permute-start.18 = (bf16[192,256]{1,0:T(8,128)(2,1)S(1)}, bf16[192,256]{1,0:T(8,128)(2,1)S(1)}, u32[]{:S(2)}, u32[]{:S(2)}) collective-permute-start(bf16[192,256]{1,0:T(8,128)(2,1)S(1)} %shard_map.111.refs_0_), channel_id=1, source_target_pairs={{0,12},{2,14},{4,8},{6,10},{8,4},{10,6},{12,0},{14,2},{1,13},{3,15... | collective-permute-start | bytes 294920 | tf_op jit(solution)/shard_map/ppermute | solution.py:339
  92.8 1.4 %copy-done.8 = bf16[4,752,256]{2,1,0:T(8,128)(2,1)S(1)} copy-done((bf16[4,752,256]{2,1,0:T(8,128)(2,1)S(1)}, bf16[4,752,256]{2,1,0:T(8,128)(2,1)}, u32[]{:S(2)}) %copy-start.8) | copy-done | bytes 1540120
  94.2 2.8 %shard_map.107 = bf16[4,720,256]{2,1,0:T(8,128)(2,1)} custom-call(s32[6]{0:T(128)S(1)} %stack.23.refs_0_.info_ref, bf16[4,752,256]{2,1,0:T(8,128)(2,1)S(1)} %copy-done.8, bf16[752,256]{1,0:T(8,128)(2,1)S(1)} %collective-permute-done.9.refs_2_.refs_0_, bf16[752,256]{1,0:T(8,128)(2,1)S(1)} %collective-permute-done.10.refs_3_.refs_1_, ...), custom_call_target="tpu_custom_call" | custom-call | flops 2194145280 | bytes 11796480 | tf_op jit(solution)/shard_map/pallas_call | solution.py:206
  97.1 2.4 %collective-permute-done.17.refs_2_ = bf16[192,256]{1,0:T(8,128)(2,1)S(1)} collective-permute-done((bf16[192,256]{1,0:T(8,128)(2,1)S(1)}, bf16[192,256]{1,0:T(8,128)(2,1)S(1)}, u32[]{:S(2)}, u32[]{:S(2)}) %collective-permute-start.17) | collective-permute-done | bytes 98336 | tf_op jit(solution)/shard_map/ppermute | solution.py:339
  99.5 0.5 collective-permute-start.20
  100.0 0.0 collective-permute-start.21
  100.0 0.5 collective-permute-start.22
  100.5 0.3 collective-permute-done.19.refs_4_
  100.8 0.2 collective-permute-done.20.refs_5_
  100.9 0.4 collective-permute-done.21.refs_6_
  101.3 0.2 collective-permute-done.22.refs_7_
  101.4 1.8 %shard_map.112 = (f32[768,256]{1,0:T(8,128)}, f32[768,256]{1,0:T(8,128)}) custom-call(s32[6]{0:T(128)S(1)} %stack.23.refs_0_.info_ref, bf16[192,256]{1,0:T(8,128)(2,1)S(1)} %shard_map.111.refs_0_, bf16[192,256]{1,0:T(8,128)(2,1)S(1)} %collective-permute-done.16.refs_1_, bf16[192,256]{1,0:T(8,128)(2,1)S(1)} %collective-permute-done.17.refs_2_, ...), custom_call_target="tpu_custom_call" | custom-call | flops 1 | bytes 1 | tf_op jit(solution)/shard_map/pallas_call | solution.py:244
  (41 shorter events, 0.1 us)
Async XLA Ops:
  0.6 8.6 %copy-start = (bf16[4,720,256]{2,1,0:T(8,128)(2,1)S(1)}, bf16[4,720,256]{2,1,0:T(8,128)(2,1)}, u32[]{:S(2)}) copy-start(bf16[4,720,256]{2,1,0:T(8,128)(2,1)} %refs_1_.1) | copy-start | bytes 4423684
  0.6 9.2 %copy-start.11 = (s32[4]{0:T(128)S(1)}, s32[4]{0:T(128)}, u32[]{:S(2)}) copy-start(s32[4]{0:T(128)} %param.9) | copy-start | bytes 52
  0.7 9.3 %copy-start.10 = (bf16[4,3,3,17]{3,0,2,1:T(4,128)(2,1)S(1)}, bf16[4,3,3,17]{3,0,2,1:T(4,128)(2,1)}, u32[]{:S(2)}) copy-start(bf16[4,3,3,17]{3,0,2,1:T(4,128)(2,1)} %param.10) | copy-start | bytes 3676
  3.5 20.2 %collective-permute-start = (bf16[720,256]{1,0:T(8,128)(2,1)}, bf16[720,256]{1,0:T(8,128)(2,1)S(1)}, u32[]{:S(2)}, u32[]{:S(2)}) collective-permute-start(bf16[720,256]{1,0:T(8,128)(2,1)} %get-tuple-element.57), channel_id=1, source_target_pairs={{0,2},{2,0},{4,6},{6,4},{8,10},{10,8},{12,14},{14,12},{1,3},{3,1},... | collective-permute-start | bytes 1105928 | tf_op jit(solution)/shard_map/ppermute | solution.py:321
  6.4 17.2 %collective-permute-start.1 = (bf16[720,256]{1,0:T(8,128)(2,1)}, bf16[720,256]{1,0:T(8,128)(2,1)}, u32[]{:S(2)}, u32[]{:S(2)}) collective-permute-start(bf16[720,256]{1,0:T(8,128)(2,1)} %get-tuple-element.56), channel_id=1, source_target_pairs={{2,4},{4,2},{6,8},{8,6},{10,12},{12,10},{3,5},{5,3},{7,9},{9,7},{1... | collective-permute-start | bytes 1105928 | tf_op jit(solution)/shard_map/ppermute | solution.py:325
  9.2 20.6 %collective-permute-start.2 = (bf16[4,32,256]{2,1,0:T(8,128)(2,1)}, bf16[4,32,256]{2,1,0:T(8,128)(2,1)S(1)}, u32[]{:S(2)}, u32[]{:S(2)}) collective-permute-start(bf16[4,32,256]{2,1,0:T(8,128)(2,1)} %pad_maximum_fusion), channel_id=1, source_target_pairs={{0,1},{1,0},{2,3},{3,2},{4,5},{5,4},{6,7},{7,6},{8,9},{9,8},{10,11... | collective-permute-start | bytes 196616 | tf_op jit(solution)/shard_map/ppermute | solution.py:333
  9.3 1.9 %collective-permute-start.6 = (bf16[4,32,256]{2,1,0:T(8,128)(2,1)S(1)}, bf16[4,32,256]{2,1,0:T(8,128)(2,1)S(1)}, u32[]{:S(2)}, u32[]{:S(2)}) collective-permute-start(bf16[4,32,256]{2,1,0:T(8,128)(2,1)S(1)} %pad_maximum_fusion.1), channel_id=1, source_target_pairs={{0,1},{1,0},{2,3},{3,2},{4,5},{5,4},{6,7},{7,6},{8,9},{9,8},{10,11... | collective-permute-start | bytes 196616 | tf_op jit(solution)/shard_map/ppermute | solution.py:333
  12.6 15.3 %copy-start.9 = (bf16[4,3,240]{2,1,0:T(4,128)(2,1)S(1)}, bf16[4,3,240]{2,1,0:T(4,128)(2,1)}, u32[]{:S(2)}) copy-start(bf16[4,3,240]{2,1,0:T(4,128)(2,1)} %reshape.70) | copy-start | bytes 17284
  12.6 17.2 %copy-start.2 = (bf16[4,720,256]{2,1,0:T(8,128)(2,1)S(1)}, bf16[4,720,256]{2,1,0:T(8,128)(2,1)}, u32[]{:S(2)}) copy-start(bf16[4,720,256]{2,1,0:T(8,128)(2,1)} %refs_1_) | copy-start | bytes 4423684
  12.6 27.7 %collective-permute-start.7 = (bf16[768,256]{1,0:T(8,128)(2,1)}, bf16[768,256]{1,0:T(8,128)(2,1)}, u32[]{:S(2)}, u32[]{:S(2)}) collective-permute-start(bf16[768,256]{1,0:T(8,128)(2,1)} %shard_map.104), channel_id=1, source_target_pairs={{0,2},{2,0},{4,6},{6,4},{8,10},{10,8},{12,14},{14,12},{1,3},{3,1},... | collective-permute-start | bytes 1179656 | tf_op jit(solution)/shard_map/ppermute | solution.py:321
  25.1 15.3 %collective-permute-start.8 = (bf16[768,256]{1,0:T(8,128)(2,1)}, bf16[768,256]{1,0:T(8,128)(2,1)}, u32[]{:S(2)}, u32[]{:S(2)}) collective-permute-start(bf16[768,256]{1,0:T(8,128)(2,1)} %shard_map.105), channel_id=1, source_target_pairs={{2,4},{4,2},{6,8},{8,6},{10,12},{12,10},{3,5},{5,3},{7,9},{9,7},{1... | collective-permute-start | bytes 1179656 | tf_op jit(solution)/shard_map/ppermute | solution.py:325
  27.9 1.9 %collective-permute-start.3 = (bf16[64,256]{1,0:T(8,128)(2,1)}, bf16[64,256]{1,0:T(8,128)(2,1)S(1)}, u32[]{:S(2)}, u32[]{:S(2)}) collective-permute-start(bf16[64,256]{1,0:T(8,128)(2,1)} %pad_maximum_fusion.2), channel_id=1, source_target_pairs={{0,1},{1,0},{2,3},{3,2},{4,5},{5,4},{6,7},{7,6},{8,9},{9,8},{10,11... | collective-permute-start | bytes 98312 | tf_op jit(solution)/shard_map/ppermute | solution.py:333
  29.8 1.0 copy-start.4
  30.8 9.6 %copy-start.6 = (bf16[3,256,256]{2,1,0:T(8,128)(2,1)S(1)}, bf16[3,256,256]{2,1,0:T(8,128)(2,1)}, u32[]{:S(2)}) copy-start(bf16[3,256,256]{2,1,0:T(8,128)(2,1)} %copy.19) | copy-start | bytes 1179652
  33.1 22.7 %collective-permute-start.4 = (bf16[752,256]{1,0:T(8,128)(2,1)S(1)}, bf16[752,256]{1,0:T(8,128)(2,1)S(1)}, u32[]{:S(2)}, u32[]{:S(2)}) collective-permute-start(bf16[752,256]{1,0:T(8,128)(2,1)S(1)} %get-tuple-element.31), channel_id=1, source_target_pairs={{0,2},{2,0},{4,6},{6,4},{8,10},{10,8},{12,14},{14,12},{1,3},{3,1},... | collective-permute-start | bytes 1155080 | tf_op jit(solution)/shard_map/ppermute | solution.py:321
  37.5 18.2 %collective-permute-start.5 = (bf16[752,256]{1,0:T(8,128)(2,1)S(1)}, bf16[752,256]{1,0:T(8,128)(2,1)S(1)}, u32[]{:S(2)}, u32[]{:S(2)}) collective-permute-start(bf16[752,256]{1,0:T(8,128)(2,1)S(1)} %get-tuple-element.32), channel_id=1, source_target_pairs={{2,4},{4,2},{6,8},{8,6},{10,12},{12,10},{3,5},{5,3},{7,9},{9,7},{1... | collective-permute-start | bytes 1155080 | tf_op jit(solution)/shard_map/ppermute | solution.py:325
  44.6 27.5 %copy-start.7 = (bf16[4,752,256]{2,1,0:T(8,128)(2,1)}, bf16[4,752,256]{2,1,0:T(8,128)(2,1)S(1)}, u32[]{:S(2)}) copy-start(bf16[4,752,256]{2,1,0:T(8,128)(2,1)S(1)} %get-tuple-element.36.refs_1_) | copy-start | bytes 4620292
  44.6 24.6 %copy-start.3 = (bf16[3,256,256]{2,1,0:T(8,128)(2,1)S(1)}, bf16[3,256,256]{2,1,0:T(8,128)(2,1)}, u32[]{:S(2)}) copy-start(bf16[3,256,256]{2,1,0:T(8,128)(2,1)} %param.12) | copy-start | bytes 1179652
  56.3 7.1 %collective-permute-start.11 = (bf16[768,256]{1,0:T(8,128)(2,1)S(1)}, bf16[768,256]{1,0:T(8,128)(2,1)S(1)}, u32[]{:S(2)}, u32[]{:S(2)}) collective-permute-start(bf16[768,256]{1,0:T(8,128)(2,1)S(1)} %shard_map.108), channel_id=1, source_target_pairs={{0,1},{1,0},{2,3},{3,2},{4,5},{5,4},{6,7},{7,6},{8,9},{9,8},{10,11... | collective-permute-start | bytes 1179656 | tf_op jit(solution)/shard_map/ppermute | solution.py:333
  56.4 27.0 %collective-permute-start.10 = (bf16[752,256]{1,0:T(8,128)(2,1)}, bf16[752,256]{1,0:T(8,128)(2,1)S(1)}, u32[]{:S(2)}, u32[]{:S(2)}) collective-permute-start(bf16[752,256]{1,0:T(8,128)(2,1)} %get-tuple-element.38), channel_id=1, source_target_pairs={{2,4},{4,2},{6,8},{8,6},{10,12},{12,10},{3,5},{5,3},{7,9},{9,7},{1... | collective-permute-start | bytes 1155080 | tf_op jit(solution)/shard_map/ppermute | solution.py:325
  57.1 26.3 %collective-permute-start.9 = (bf16[752,256]{1,0:T(8,128)(2,1)}, bf16[752,256]{1,0:T(8,128)(2,1)S(1)}, u32[]{:S(2)}, u32[]{:S(2)}) collective-permute-start(bf16[752,256]{1,0:T(8,128)(2,1)} %get-tuple-element.37), channel_id=1, source_target_pairs={{0,2},{2,0},{4,6},{6,4},{8,10},{10,8},{12,14},{14,12},{1,3},{3,1},... | collective-permute-start | bytes 1155080 | tf_op jit(solution)/shard_map/ppermute | solution.py:321
  64.0 10.1 %collective-permute-start.12 = (bf16[192,256]{1,0:T(8,128)(2,1)S(1)}, bf16[192,256]{1,0:T(8,128)(2,1)S(1)}, u32[]{:S(2)}, u32[]{:S(2)}) collective-permute-start(bf16[192,256]{1,0:T(8,128)(2,1)S(1)} %get-tuple-element.43), channel_id=1, source_target_pairs={{0,4},{2,6},{4,0},{6,2},{8,12},{10,14},{12,8},{14,10},{1,5},{3,7},... | collective-permute-start | bytes 294920 | tf_op jit(solution)/shard_map/ppermute | solution.py:339
  66.8 9.3 %collective-permute-start.13 = (bf16[192,256]{1,0:T(8,128)(2,1)S(1)}, bf16[192,256]{1,0:T(8,128)(2,1)S(1)}, u32[]{:S(2)}, u32[]{:S(2)}) collective-permute-start(bf16[192,256]{1,0:T(8,128)(2,1)S(1)} %get-tuple-element.44), channel_id=1, source_target_pairs={{0,8},{2,10},{4,12},{6,14},{8,0},{10,2},{12,4},{14,6},{1,9},{3,11}... | collective-permute-start | bytes 294920 | tf_op jit(solution)/shard_map/ppermute | solution.py:339
  66.8 14.3 %collective-permute-start.14 = (bf16[192,256]{1,0:T(8,128)(2,1)S(1)}, bf16[192,256]{1,0:T(8,128)(2,1)S(1)}, u32[]{:S(2)}, u32[]{:S(2)}) collective-permute-start(bf16[192,256]{1,0:T(8,128)(2,1)S(1)} %get-tuple-element.45), channel_id=1, source_target_pairs={{0,12},{2,14},{4,8},{6,10},{8,4},{10,6},{12,0},{14,2},{1,13},{3,15... | collective-permute-start | bytes 294920 | tf_op jit(solution)/shard_map/ppermute | solution.py:339
  69.3 13.9 %copy-start.5 = (bf16[3,256,256]{2,1,0:T(8,128)(2,1)S(1)}, bf16[3,256,256]{2,1,0:T(8,128)(2,1)}, u32[]{:S(2)}) copy-start(bf16[3,256,256]{2,1,0:T(8,128)(2,1)} %param.11) | copy-start | bytes 1179652
  81.1 1.4 %copy-start.1 = (bf16[4,720,256]{2,1,0:T(8,128)(2,1)S(1)}, bf16[4,720,256]{2,1,0:T(8,128)(2,1)}, u32[]{:S(2)}) copy-start(bf16[4,720,256]{2,1,0:T(8,128)(2,1)} %shard_map.103.refs_0_) | copy-start | bytes 4423684
  83.1 4.7 %collective-permute-start.15 = (bf16[192,256]{1,0:T(8,128)(2,1)S(1)}, bf16[192,256]{1,0:T(8,128)(2,1)S(1)}, u32[]{:S(2)}, u32[]{:S(2)}) collective-permute-start(bf16[192,256]{1,0:T(8,128)(2,1)S(1)} %shard_map.110.refs_2_), channel_id=1, source_target_pairs={{0,2},{2,0},{4,6},{6,4},{8,10},{10,8},{12,14},{14,12},{1,3},{3,1},... | collective-permute-start | bytes 294920 | tf_op jit(solution)/shard_map/ppermute | solution.py:354
  88.4 8.7 %collective-permute-start.16 = (bf16[192,256]{1,0:T(8,128)(2,1)S(1)}, bf16[192,256]{1,0:T(8,128)(2,1)S(1)}, u32[]{:S(2)}, u32[]{:S(2)}) collective-permute-start(bf16[192,256]{1,0:T(8,128)(2,1)S(1)} %shard_map.111.refs_0_), channel_id=1, source_target_pairs={{0,4},{2,6},{4,0},{6,2},{8,12},{10,14},{12,8},{14,10},{1,5},{3,7},... | collective-permute-start | bytes 294920 | tf_op jit(solution)/shard_map/ppermute | solution.py:339
  90.1 9.3 %collective-permute-start.17 = (bf16[192,256]{1,0:T(8,128)(2,1)S(1)}, bf16[192,256]{1,0:T(8,128)(2,1)S(1)}, u32[]{:S(2)}, u32[]{:S(2)}) collective-permute-start(bf16[192,256]{1,0:T(8,128)(2,1)S(1)} %shard_map.111.refs_0_), channel_id=1, source_target_pairs={{0,8},{2,10},{4,12},{6,14},{8,0},{10,2},{12,4},{14,6},{1,9},{3,11}... | collective-permute-start | bytes 294920 | tf_op jit(solution)/shard_map/ppermute | solution.py:339
  90.9 8.6 %collective-permute-start.18 = (bf16[192,256]{1,0:T(8,128)(2,1)S(1)}, bf16[192,256]{1,0:T(8,128)(2,1)S(1)}, u32[]{:S(2)}, u32[]{:S(2)}) collective-permute-start(bf16[192,256]{1,0:T(8,128)(2,1)S(1)} %shard_map.111.refs_0_), channel_id=1, source_target_pairs={{0,12},{2,14},{4,8},{6,10},{8,4},{10,6},{12,0},{14,2},{1,13},{3,15... | collective-permute-start | bytes 294920 | tf_op jit(solution)/shard_map/ppermute | solution.py:339
  92.8 1.4 %copy-start.8 = (bf16[4,752,256]{2,1,0:T(8,128)(2,1)S(1)}, bf16[4,752,256]{2,1,0:T(8,128)(2,1)}, u32[]{:S(2)}) copy-start(bf16[4,752,256]{2,1,0:T(8,128)(2,1)} %copy-done.7) | copy-start | bytes 4620292
  99.5 1.3 %collective-permute-start.19 = (bf16[192,256]{1,0:T(8,128)(2,1)S(1)}, bf16[192,256]{1,0:T(8,128)(2,1)S(1)}, u32[]{:S(2)}, u32[]{:S(2)}) collective-permute-start(bf16[192,256]{1,0:T(8,128)(2,1)S(1)} %shard_map.111.refs_0_), channel_id=1, source_target_pairs={{0,1},{1,0},{2,3},{3,2},{4,5},{5,4},{6,7},{7,6},{8,9},{9,8},{10,11... | collective-permute-start | bytes 294920 | tf_op jit(solution)/shard_map/ppermute | solution.py:333
  99.5 1.5 %collective-permute-start.20 = (bf16[192,256]{1,0:T(8,128)(2,1)S(1)}, bf16[192,256]{1,0:T(8,128)(2,1)S(1)}, u32[]{:S(2)}, u32[]{:S(2)}) collective-permute-start(bf16[192,256]{1,0:T(8,128)(2,1)S(1)} %collective-permute-done.16.refs_1_), channel_id=1, source_target_pairs={{0,1},{1,0},{2,3},{3,2},{4,5},{5,4},{6,7},{7,6},{8,9},{9,8},{10,11... | collective-permute-start | bytes 294920 | tf_op jit(solution)/shard_map/ppermute | solution.py:333
  100.0 1.3 %collective-permute-start.21 = (bf16[192,256]{1,0:T(8,128)(2,1)S(1)}, bf16[192,256]{1,0:T(8,128)(2,1)S(1)}, u32[]{:S(2)}, u32[]{:S(2)}) collective-permute-start(bf16[192,256]{1,0:T(8,128)(2,1)S(1)} %collective-permute-done.17.refs_2_), channel_id=1, source_target_pairs={{0,1},{1,0},{2,3},{3,2},{4,5},{5,4},{6,7},{7,6},{8,9},{9,8},{10,11... | collective-permute-start | bytes 294920 | tf_op jit(solution)/shard_map/ppermute | solution.py:333
  100.0 1.5 %collective-permute-start.22 = (bf16[192,256]{1,0:T(8,128)(2,1)S(1)}, bf16[192,256]{1,0:T(8,128)(2,1)S(1)}, u32[]{:S(2)}, u32[]{:S(2)}) collective-permute-start(bf16[192,256]{1,0:T(8,128)(2,1)S(1)} %collective-permute-done.18.refs_3_), channel_id=1, source_target_pairs={{0,1},{1,0},{2,3},{3,2},{4,5},{5,4},{6,7},{7,6},{8,9},{9,8},{10,11... | collective-permute-start | bytes 294920 | tf_op jit(solution)/shard_map/ppermute | solution.py:333

commit v2 on v1

--- a/solution.py
+++ b/solution.py
@@ -24,21 +24,26 @@
     return pl.CostEstimate(flops=flops, bytes_accessed=bytes_accessed, transcendentals=0)
 
 
-def stage_kernel(mode, scale, *refs):
-    info_ref, x_ref, ev_ref, od_ref, mix_ref = refs[:5]
+def stage_kernel(mode, transposed, scale, *refs):
+    info_ref, x_ref, mix_ref = refs[:3]
     slots, channels = x_ref.shape[0], x_ref.shape[2]
-    wide = ev_ref.shape[0] + {"first": 2 * EDGE, "back": -EDGE, "last": 0}[mode]
+    wide = x_ref.shape[1] + (0 if mode == "last" else 2 * EDGE)
     lon_count = wide - 2 * EDGE
+    back = mode in ("inner", "outer")
     height, odd = info_ref[0], info_ref[1]
     own = slice(EDGE, EDGE + lon_count)
     if mode == "first":
-        edge_ref, halo_ref, coef_ref, basis_ref, out_ref, slope_ref, ev_out, od_out, band_ref, xe_ref = refs[5:]
-    elif mode == "back":
-        edge_ref, coef_ref, slope_ref, basis_ref, hidden_ref = refs[5:10]
-        out_ref, ext_ref, ev_out, od_out, mine_ref, other_ref = refs[10:16]
-        band_ref, terms_ref, xe_ref, acc_one, acc_two = refs[16:]
+        ev_ref, od_ref, edge_ref, halo_ref, coef_ref, basis_ref, out_ref, slope_ref, ev_out, od_out = refs[3:13]
+        band_ref, xe_ref = refs[13:]
+    elif mode == "inner":
+        edge_ref, coef_ref, slope_ref, basis_ref, hidden_ref = refs[3:8]
+        out_ref, acc_one, acc_two, band_ref, terms_ref, xe_ref, ext_ref = refs[8:]
+    elif mode == "outer":
+        ev_ref, od_ref, edge_ref, coef_ref, slope_ref, basis_ref, hidden_ref, _, one_ref, two_ref = refs[3:13]
+        out_ref, ext_ref, ev_out, od_out, mine_ref, other_ref = refs[13:19]
+        band_ref, terms_ref, xe_ref, acc_one, acc_two = refs[19:]
     else:
-        coef_ref, out_ref, band_ref, terms_ref, xe_ref = refs[5:]
+        ev_ref, od_ref, coef_ref, out_ref, token_ref, band_ref, terms_ref, xe_ref = refs[3:]
 
     def each_live(act):
         def step(row, carry):
@@ -62,31 +67,49 @@
             xe_ref[slot, EDGE + lon_count : wide, :] = halo_ref[at : at + EDGE, :]
         else:
             xe_ref[slot] = src_ref[0:wide, :]
-        if mode == "back":
+        if mode == "outer":
             ext_ref[slot] = src_ref[wide : wide + EDGE, :].astype(jnp.float32)[0:8]
 
     each_live(load)
-    if mode == "back":
+    if back:
         ext_ref[1 : slots + 1] = coef_ref[...]
+    if mode == "inner":
         acc_one[...] = jnp.zeros_like(acc_one)
         acc_two[...] = jnp.zeros_like(acc_two)
-
-    @pl.when(odd == 1)
-    def _():
-        load_halo(ev_ref, 0, 0)
-        load_halo(od_ref, 2 * EDGE, height + 1)
-
-    @pl.when(odd == 0)
-    def _():
-        load_halo(od_ref, 2 * EDGE, 0)
-        load_halo(ev_ref, 0, height + 1)
+    if mode == "outer":
+        acc_one[...] = one_ref[...]
+        acc_two[...] = two_ref[...]
+
+    if mode != "inner":
+
+        @pl.when(odd == 1)
+        def _():
+            load_halo(ev_ref, 0, 0)
+            load_halo(od_ref, 2 * EDGE, height + 1)
+
+        @pl.when(odd == 0)
+        def _():
+            load_halo(od_ref, 2 * EDGE, 0)
+            load_halo(ev_ref, 0, height + 1)
+
+    def mix(terms):
+        if not transposed:
+            return jnp.dot(terms, mix_ref[...], preferred_element_type=jnp.float32)
+        total = None
+        for k in range(3):
+            span = slice(k * channels, (k + 1) * channels)
+            part = lax.dot_general(
+                terms[:, span], mix_ref[span, :], (((1,), (1,)), ((), ())), preferred_element_type=jnp.float32
+            )
+            total = part if total is None else total + part
+        return total
 
     zeros_tail = jnp.zeros((LANES - 3 * WINDOW, channels), jnp.bfloat16)
     tiles = lon_count // TILE
     chunk = -(-tiles // CHUNKS)
 
     def one_row(row):
-        rows_ref = ext_ref if mode == "back" else coef_ref
+        rows_ref = ext_ref if back else coef_ref
         if rows_ref.shape[0] == slots:
             base = rows_ref[row]
         else:
@@ -130,20 +153,20 @@
                     else:
                         terms_ref[at : at + size, span] = piece
             terms = basis_ref[row, begin:end, :] if mode == "first" else terms_ref[begin:end, :]
-            mixed = jnp.dot(terms, mix_ref[...], preferred_element_type=jnp.float32)
+            mixed = mix(terms)
             if mode == "first":
                 cdf = 0.5 * (1.0 + lax.erf(mixed * (1.0 / math.sqrt(2.0))))
                 pdf = jnp.exp(-0.5 * mixed * mixed) * (1.0 / math.sqrt(2.0 * math.pi))
                 out_ref[row, begin:end, :] = (mixed * cdf).astype(jnp.bfloat16)
                 slope_ref[row, begin:end, :] = cdf + mixed * pdf
-            elif mode == "back":
+            elif back:
                 out_ref[row, begin:end, :] = (mixed * slope_ref[row, begin:end, :]).astype(jnp.bfloat16)
             else:
                 out_ref[row, begin - EDGE : end - EDGE, :] = mixed.astype(jnp.bfloat16)
 
         for first_tile in range(0, tiles, chunk):
             emit(first_tile, min(first_tile + chunk, tiles))
-        if mode == "back":
+        if back:
             grad_t = out_ref[row, own, :].T
             hidden_t = hidden_ref[row, own, :].T
             for k in range(3):
@@ -151,7 +174,22 @@
                 acc_one[:, span] += jnp.dot(grad_t, basis_ref[row, own, span], preferred_element_type=jnp.float32)
                 acc_two[:, span] += jnp.dot(hidden_t, terms_ref[own, span], preferred_element_type=jnp.float32)
 
-    each_live(one_row)
+    if mode == "inner":
+
+        def inner_row(row, carry):
+            one_row(row)
+            return carry
+
+        lax.fori_loop(1, height - 1, inner_row, 0)
+    elif mode == "outer":
+
+        def outer_row(end, carry):
+            one_row(end * (height - 1))
+            return carry
+
+        lax.fori_loop(0, jnp.minimum(height, 2), outer_row, 0)
+    else:
+        each_live(one_row)
     if mode == "last":
 
         def clear(row, carry):
@@ -159,10 +197,11 @@
             return carry
 
         lax.fori_loop(height, slots, clear, 0)
-    else:
+        token_ref[...] = jnp.zeros_like(token_ref)
+    elif mode != "inner":
         ev_out[...] = out_ref[info_ref[2]]
         od_out[...] = out_ref[info_ref[3]]
-        if mode == "back":
+        if mode == "outer":
 
             def write(one_ref, two_ref):
                 for k in range(3):
@@ -179,9 +218,9 @@
                 write(other_ref, mine_ref)
 
 
-def stage(mode, estimate, info, x, ev, od, mix, *extra, scale=None):
+def stage(mode, estimate, info, x, mix, *extra, transposed=False, scale=None):
     slots, channels = x.shape[0], x.shape[2]
-    wide = ev.shape[0] + {"first": 2 * EDGE, "back": -EDGE, "last": 0}[mode]
+    wide = x.shape[1] + (0 if mode == "last" else 2 * EDGE)
     lon_count = wide - 2 * EDGE
     bf16, f32 = jnp.bfloat16, jnp.float32
     vmem = pl.BlockSpec(memory_space=pltpu.VMEM)
@@ -193,25 +232,41 @@
     terms = ((wide, 3 * channels), bf16)
     ext = ((slots + 2, wide, channels), bf16)
     sums = (3 * channels, channels)
+    ext_coef = ((slots + 2, 8, LANES), f32)
+    acc = ((channels, 3 * channels), f32)
     if mode == "first":
         outs = (basis, field, slope, row, row)
         scratch = [band, ext]
-    elif mode == "back":
-        outs = (field, ((slots + 2, 8, LANES), f32), row, row, (sums, f32), (sums, bf16))
-        acc = ((channels, 3 * channels), f32)
+    elif mode == "inner":
+        outs = (field, acc, acc)
+        scratch = [band, terms, ext, ext_coef]
+    elif mode == "outer":
+        outs = (field, ext_coef, row, row, (sums, f32), (sums, bf16))
         scratch = [band, terms, ext, acc, acc]
     else:
-        outs = (((slots, lon_count, channels), bf16),)
+        outs = (((slots, lon_count, channels), bf16), ((8, 128), f32))
         scratch = [band, terms, ext]
     return pl.pallas_call(
-        functools.partial(stage_kernel, mode, scale),
+        functools.partial(stage_kernel, mode, transposed, scale),
         out_shape=tuple(jax.ShapeDtypeStruct(*array) for array in outs),
-        in_specs=[pl.BlockSpec(memory_space=pltpu.SMEM)] + [vmem] * (4 + len(extra)),
+        in_specs=[pl.BlockSpec(memory_space=pltpu.SMEM)] + [vmem] * (2 + len(extra)),
         out_specs=(vmem,) * len(outs),
         scratch_shapes=[pltpu.VMEM(*array) for array in scratch],
+        input_output_aliases={10: 0} if mode == "outer" else {},
         compiler_params=pltpu.CompilerParams(vmem_limit_bytes=VMEM_LIMIT),
         cost_estimate=estimate,
-    )(info, x, ev, od, mix, *extra)
+    )(info, x, mix, *extra)
+
+
+def edge_kernel(info_ref, x_ref, out_ref):
+    lon_count = x_ref.shape[1]
+    out_ref[:, 0:EDGE, :] = x_ref[:, 0:EDGE, :]
+    out_ref[:, EDGE : 2 * EDGE, :] = x_ref[:, lon_count - EDGE :, :]
+
+
+def row_edges(info, x):
+    out = jax.ShapeDtypeStruct((x.shape[0], 2 * EDGE, x.shape[2]), x.dtype)
+    return local_call(edge_kernel, info, (out,), SMALL_LIMIT, cost(1, 4 * x.size), (x,))[0]
 
 
 def pack_kernel(which, info_ref, x_ref, edge_ref, tile_ref, out_ref, sem):
@@ -254,13 +309,21 @@
     )(info, *after, *far, *operands)
 
 
-def pass_kernel(info_ref, value_ref, out_ref):
-    out_ref[...] = value_ref[...]
-
-
-def pass_after(info, value, after):
-    (out,) = local_call(pass_kernel, info, (jax.ShapeDtypeStruct(value.shape, value.dtype),), SMALL_LIMIT, cost(1, 1), (value,), after=after)
-    return out
+def gate_kernel(*refs):
+    pass
+
+
+def gate(value, after):
+    anywhere = pl.BlockSpec(memory_space=pl.ANY)
+    return pl.pallas_call(
+        gate_kernel,
+        out_shape=jax.ShapeDtypeStruct(value.shape, value.dtype),
+        in_specs=[anywhere] * (1 + len(after)),
+        out_specs=anywhere,
+        input_output_aliases={0: 0},
+        compiler_params=pltpu.CompilerParams(vmem_limit_bytes=SMALL_LIMIT),
+        cost_estimate=cost(1, 1),
+    )(value, *after)
 
 
 def sum_kernel(info_ref, *refs):
@@ -270,7 +333,7 @@
     refs[-1][...] = total.astype(jnp.bfloat16)
 
 
-def rounded_sum(info, terms, after):
+def rounded_sum(info, terms, after=()):
     out = jax.ShapeDtypeStruct(terms[0].shape, jnp.bfloat16)
     return local_call(sum_kernel, info, (out,), SMALL_LIMIT, cost(1, 1), terms, after=after)[0]
 
@@ -346,14 +409,18 @@
     return own, sends
 
 
-def total(info, own, sends, before_swap, before_gather, before_join):
+def lat_sum(info, own, heard, before_first, before_last):
     size = lax.axis_size("lat")
-    held = rounded_sum(info, [own] + [across(sends[step - 1], step) for step in (1, 2, 3)], before_swap)
+    held = rounded_sum(info, [own] + heard, before_first)
     stride = 1
     while stride < size // 4:
-        heard = lax.ppermute(held, "lat", [(i, i ^ stride) for i in range(size)])
+        term = lax.ppermute(held, "lat", [(i, i ^ stride) for i in range(size)])
         stride *= 2
-        held = rounded_sum(info, [held, heard], before_gather if stride == size // 4 else ())
+        held = rounded_sum(info, [held, term], before_last if stride == size // 4 else ())
+    return held
+
+
+def gather(info, held, before_join):
     pieces = [held] + [across(held, step) for step in (1, 2, 3)]
     pieces, _ = lax.optimization_barrier((pieces, before_join))
     pieces += [partner(value) for value in pieces]
@@ -385,33 +452,37 @@
     backward_tile = jnp.pad(backward, ((0, 0), (0, EDGE - 8), (0, 0)))
     mix_one = weights_one.reshape(3 * channels, channels)
     mix_two = weights_two.reshape(3 * channels, channels)
-    mix_one_t = jnp.swapaxes(weights_one, 1, 2).reshape(3 * channels, channels)
-    mix_two_t = jnp.swapaxes(weights_two, 1, 2).reshape(3 * channels, channels)
-
-    edges_s = partner(edge_columns(state_field))
-    edges_c = partner(edge_columns(cotangent))
+
+    edges_s = partner(row_edges(info, state_field))
+    edges_c = partner(row_edges(info, cotangent))
     cot_ev = ev_swap(pack(2, info, cotangent, edges_c, backward_tile))
-    cot_od = od_swap(pack(3, info, cotangent, edges_c, backward_tile, (state_ev, state_od)))
+    cot_od = od_swap(gate(pack(3, info, cotangent, edges_c, backward_tile), (state_ev, state_od)))
     halo_edges = partner(jnp.concatenate([edge_columns(state_ev), edge_columns(state_od)], axis=0))
 
     points = state_field.shape[0] * state_field.shape[1]
     flops = 2 * points * channels * (9 * WINDOW + 3 * channels)
     full, most = cost(flops, points * channels * 16), cost(3 * flops, points * channels * 24)
     basis_one, hidden, slope, ev, od = stage(
-        "first", full, info, state_field, state_ev, state_od, mix_one, edges_s, halo_edges, forward
-    )
-    hidden_ev, hidden_od = row_swap(ev, od)
+        "first", full, info, state_field, mix_one, state_ev, state_od, edges_s, halo_edges, forward
+    )
+    hidden_ev, hidden_od = ev_swap(ev), od_swap(gate(od, (cot_ev, cot_od)))
     scale = 1.0 / math.sqrt(ROWS * lax.axis_size("lat") * NLON)
+    backward_wide = backward.astype(jnp.float32)
+    grad_inner, inner_one, inner_two = stage(
+        "inner", cost(1, 1), info, cotangent, mix_two, edges_c, backward_wide, slope, basis_one, hidden, transposed=True, scale=scale
+    )
     grad_pre, backward_ext, ev, od, mine, other = stage(
-        "back", most, info, cotangent, cot_ev, cot_od, mix_two_t, edges_c, backward.astype(jnp.float32),
-        slope, basis_one, hidden, scale=scale,
-    )
-    other = pass_after(info, other, (hidden_ev, hidden_od))
-    own, sends = cut_terms(info, mine, other)
-    grad_ev, grad_od = row_swap(ev, od)
-    (next_field,) = stage("last", full, info, hidden, hidden_ev, hidden_od, mix_two, forward)
-    (grad_field,) = stage("last", full, info, grad_pre, grad_ev, grad_od, mix_one_t, backward_ext)
-    grad_one, grad_two = total(info, own, sends, (next_field,), (grad_ev, grad_od), grad_field)
+        "outer", most, info, cotangent, mix_two, cot_ev, cot_od, edges_c, backward_wide, slope, basis_one, hidden,
+        grad_inner, inner_one, inner_two, transposed=True, scale=scale,
+    )
+    own, sends = cut_terms(info, mine, gate(other, (hidden_od,)))
+    heard = [across(send, step) for send, step in zip(sends, (1, 2, 3), strict=True)]
+    grad_ev = ev_swap(ev)
+    grad_od = od_swap(gate(od, heard))
+    next_field, next_token = stage("last", full, info, hidden, mix_two, hidden_ev, hidden_od, forward)
+    held = lat_sum(info, own, heard, (), (next_token, grad_ev, grad_od))
+    grad_field, grad_token = stage("last", full, info, grad_pre, mix_one, grad_ev, grad_od, backward_ext, transposed=True)
+    grad_one, grad_two = gather(info, held, grad_field)
     return next_field, grad_field, grad_one.reshape(weights_one.shape), grad_two.reshape(weights_two.shape)
 
 

time: 103 us -> 100 us (0.971)
  local copies, waits for them, and re-layouts: 10.6 us -> 3.37 us
  starting transfers between devices: 32.9 us -> 39.1 us
  waiting for transfers between devices: 37.4 us -> 32.3 us
  Pallas kernels: 19.3 us -> 23 us
  other arithmetic: 1.35 us -> 0.11 us
    pallas_call x4 -> x9, Pallas kernels: 12.2 us -> 16.9 us  [the longest x5 16.9 us: stage(): pl.pallas_call(functools.partial(stage_kernel, mode, transposed, scale),...]
    ppermute x1, starting transfers between devices: 0.07 us -> 4.66 us  [lat_sum(): term = lax.ppermute(held, 'lat', [(i, i ^ stride) for i in range(size)])]
    unnamed x26 -> x14, local copies, waits for them, and re-layouts: 3.81 us -> 0.04 us
    ppermute x6, waiting for transfers between devices: 11.4 us -> 8.41 us  [across(): lax.ppermute(value, 'lat', [(i, (i // low ^ step) * low + i % low) for i...]
    ppermute x1, waiting for transfers between devices: 4.4 us -> 2.01 us  [lat_sum(): term = lax.ppermute(held, 'lat', [(i, i ^ stride) for i in range(size)])]
    transpose x2 -> x0, local copies, waits for them, and re-layouts: 2.09 us -> none  [the longest x1 1.92 us: per_device(): mix_two_t = jnp.swapaxes(weights_two, 1, 2).reshape(3 * channels, channels)]
    ppermute x6, starting transfers between devices: 9.66 us -> 11.5 us  [across(): lax.ppermute(value, 'lat', [(i, (i // low ^ step) * low + i % low) for i...]
    ppermute x8, waiting for transfers between devices: 0.95 us -> 2.42 us  [partner(): return lax.ppermute(value, 'lon', [(0, 1), (1, 0)])]
  transfers between devices with their start and end apart: 23 -> 23, of which waited for: 12 -> 13; matrix products, arithmetic and copies ran while one was open for 6% -> 1% of each run, Pallas kernels for 16% -> 21%
where the time goes in v2:
time: 100 us; the launch traced here: 99.6 us
  starting transfers between devices  39.1 us (39%)
  waiting for transfers between devices  32.3 us (32%)
  Pallas kernels  23 us (23%)
  local copies, waits for them, and re-layouts  3.37 us (3%)
  between operations  1.72 us (2%)
    ppermute x4, waiting for transfers between devices, ev_swap(): lax.ppermute(row, 'lat', [(i, i ^ 1) for i in range(lax.axis_size('lat'))])  19.5 us
    ppermute x4, starting transfers between devices, ev_swap(): lax.ppermute(row, 'lat', [(i, i ^ 1) for i in range(lax.axis_size('lat'))])  17.8 us
    pallas_call x5, Pallas kernels, stage(): pl.pallas_call(functools.partial(stage_kernel, mode, transposed, scale),...  16.9 us
    ppermute x6, starting transfers between devices, across(): lax.ppermute(value, 'lat', [(i, (i // low ^ step) * low + i % low) for i...  11.5 us
    ppermute x6, waiting for transfers between devices, across(): lax.ppermute(value, 'lat', [(i, (i // low ^ step) * low + i % low) for i...  8.41 us
    pallas_call x8, Pallas kernels, local_call(): pl.pallas_call(body, out_shape=tuple(outs), in_specs=[pl.BlockSpec(memory...  6.08 us
    ppermute x1, starting transfers between devices, lat_sum(): term = lax.ppermute(held, 'lat', [(i, i ^ stride) for i in range(size)])  4.66 us
    ppermute x4, starting transfers between devices, od_swap(): lax.ppermute(row, 'lat', [(i, i + 1 if i % 2 else i - 1) for i in range(1...  3.42 us
  transfers between devices with their start and end apart: 23, of which 13 were waited for; matrix products, arithmetic and copies ran while one was open for 1% of the time, Pallas kernels for 21%

profile of v2, /device:TPU:0, one launch (start us, length us, event | category | flops | bytes accessed | tf_op | source)
XLA Modules:
  0.0 99.6 jit_solution(2063411987543390438)
XLA Ops:
  1.5 2.1 %dynamic-slice_bitcast_fusion = (bf16[720,256]{1,0:T(8,128)(2,1)}, bf16[720,256]{1,0:T(8,128)(2,1)}) fusion(bf16[4,720,256]{2,1,0:T(8,128)(2,1)} %refs_1_, s32[]{:T(128)S(6)} %select_n.28, s32[]{:T(128)S(6)} %select_n.27), kind=kLoop, calls=%fused_computation | loop fusion | bytes 1474568 | tf_op jit(solution)/shard_map/jit(dynamic_index_in_dim)/squeeze | solution.py:441
  3.5 3.0 %collective-permute-start = (bf16[720,256]{1,0:T(8,128)(2,1)}, bf16[720,256]{1,0:T(8,128)(2,1)S(1)}, u32[]{:S(2)}, u32[]{:S(2)}) collective-permute-start(bf16[720,256]{1,0:T(8,128)(2,1)} %get-tuple-element.65), channel_id=1, source_target_pairs={{0,2},{2,0},{4,6},{6,4},{8,10},{10,8},{12,14},{14,12},{1,3},{3,1},... | collective-permute-start | bytes 1105928 | tf_op jit(solution)/shard_map/ppermute | solution.py:384
  6.5 1.4 %collective-permute-start.1 = (bf16[720,256]{1,0:T(8,128)(2,1)}, bf16[720,256]{1,0:T(8,128)(2,1)}, u32[]{:S(2)}, u32[]{:S(2)}) collective-permute-start(bf16[720,256]{1,0:T(8,128)(2,1)} %get-tuple-element.64), channel_id=1, source_target_pairs={{2,4},{4,2},{6,8},{8,6},{10,12},{12,10},{3,5},{5,3},{7,9},{9,7},{1... | collective-permute-start | bytes 1105928 | tf_op jit(solution)/shard_map/ppermute | solution.py:388
  7.9 0.1 stack.23.info_ref.refs_0_
  8.0 0.0 copy-start.4
  8.0 0.5 shard_map.102
  8.6 0.1 collective-permute-start.2
  8.6 0.5 shard_map.104
  9.2 0.6 collective-permute-start.5
  9.8 0.1 broadcast_compare_fusion
  9.9 0.1 rev.3
  10.0 0.1 pad.18.clone
  10.1 0.1 reshape.62
  10.2 0.1 pad.20.clone
  10.2 0.1 reshape.63
  10.4 0.3 collective-permute-done.5.refs_1_.refs_3_.refs_5_
  10.7 0.7 shard_map.105
  11.4 0.0 copy-start.3
  11.4 3.6 %collective-permute-start.6 = (bf16[768,256]{1,0:T(8,128)(2,1)S(1)}, bf16[768,256]{1,0:T(8,128)(2,1)S(1)}, u32[]{:S(2)}, u32[]{:S(2)}) collective-permute-start(bf16[768,256]{1,0:T(8,128)(2,1)S(1)} %shard_map.105), channel_id=1, source_target_pairs={{0,2},{2,0},{4,6},{6,4},{8,10},{10,8},{12,14},{14,12},{1,3},{3,1},... | collective-permute-start | bytes 1179656 | tf_op jit(solution)/shard_map/ppermute | solution.py:384
  15.0 0.7 shard_map.106.refs_0_
  15.7 8.0 %collective-permute-done.refs_3_.refs_1_ = bf16[720,256]{1,0:T(8,128)(2,1)S(1)} collective-permute-done((bf16[720,256]{1,0:T(8,128)(2,1)}, bf16[720,256]{1,0:T(8,128)(2,1)S(1)}, u32[]{:S(2)}, u32[]{:S(2)}) %collective-permute-start) | collective-permute-done | bytes 368672 | tf_op jit(solution)/shard_map/ppermute | solution.py:384
  23.7 0.0 collective-permute-done.1.refs_4_.refs_2_
  23.7 0.7 collective-permute-start.7
  24.4 0.7 fusion.1
  25.1 0.0 collective-permute-start.3
  25.2 1.2 %collective-permute-done.3.refs_6_ = bf16[64,256]{1,0:T(8,128)(2,1)S(1)} collective-permute-done((bf16[64,256]{1,0:T(8,128)(2,1)S(1)}, bf16[64,256]{1,0:T(8,128)(2,1)S(1)}, u32[]{:S(2)}, u32[]{:S(2)}) %collective-permute-start.3) | collective-permute-done | bytes 32800 | tf_op jit(solution)/shard_map/ppermute | solution.py:396
  26.3 3.4 %shard_map.103 = (bf16[4,752,768]{2,1,0:T(8,128)(2,1)S(1)}, bf16[4,752,256]{2,1,0:T(8,128)(2,1)S(1)}, f32[4,752,256]{2,1,0:T(8,128)S(1)}, bf16[752,256]{1,0:T(8,128)(2,1)S(1)}, bf16[752,256]{1,0:T(8,128)(2,1)S(1)}) custom-call(s32[6]{0:T(128)S(1)} %stack.23.info_ref.refs_0_, bf16[4,720,256]{2,1,0:T(8,128)(2,1)S(1)} %copy-done.1, ...), custom_call_target="tpu_custom_call" | custom-call | flops 2194145280 | bytes 11796480 | tf_op jit(solution)/shard_map/pallas_call | solution.py:249
  29.8 0.7 shard_map.110
  30.5 8.8 %collective-permute-done.6.refs_1_.refs_3_ = bf16[768,256]{1,0:T(8,128)(2,1)S(1)} collective-permute-done((bf16[768,256]{1,0:T(8,128)(2,1)S(1)}, bf16[768,256]{1,0:T(8,128)(2,1)S(1)}, u32[]{:S(2)}, u32[]{:S(2)}) %collective-permute-start.6) | collective-permute-done | bytes 393248 | tf_op jit(solution)/shard_map/ppermute | solution.py:384
  39.3 0.7 collective-permute-start.8
  40.0 4.8 %shard_map.111 = (bf16[4,752,256]{2,1,0:T(8,128)(2,1)S(1)}, f32[6,8,256]{2,1,0:T(8,128)S(1)}, bf16[752,256]{1,0:T(8,128)(2,1)S(1)}, bf16[752,256]{1,0:T(8,128)(2...) custom-call(s32[6]{0:T(128)S(1)} %stack.23.info_ref.refs_0_, ...), custom_call_target="tpu_custom_call", output_to_operand_aliasing={{0}: (10, {})} | custom-call | flops 6582435840 | bytes 17694720 | tf_op jit(solution)/shard_map/pallas_call | solution.py:249
  44.8 0.0 collective-permute-done.8.refs_4_.refs_1_
  44.8 0.1 collective-permute-start.10
  44.9 9.5 %collective-permute-start.4 = (bf16[752,256]{1,0:T(8,128)(2,1)S(1)}, bf16[752,256]{1,0:T(8,128)(2,1)S(1)}, u32[]{:S(2)}, u32[]{:S(2)}) collective-permute-start(bf16[752,256]{1,0:T(8,128)(2,1)S(1)} %get-tuple-element.37), channel_id=1, source_target_pairs={{0,2},{2,0},{4,6},{6,4},{8,10},{10,8},{12,14},{14,12},{1,3},{3,1},... | collective-permute-start | bytes 1155080 | tf_op jit(solution)/shard_map/ppermute | solution.py:384
  54.4 0.0 collective-permute-done.10.refs_1_
  54.4 0.6 shard_map.113
  55.0 1.8 %collective-permute-start.11 = (bf16[192,256]{1,0:T(8,128)(2,1)S(1)}, bf16[192,256]{1,0:T(8,128)(2,1)S(1)}, u32[]{:S(2)}, u32[]{:S(2)}) collective-permute-start(bf16[192,256]{1,0:T(8,128)(2,1)S(1)} %get-tuple-element.51), channel_id=1, source_target_pairs={{0,4},{2,6},{4,0},{6,2},{8,12},{10,14},{12,8},{14,10},{1,5},{3,7},... | collective-permute-start | bytes 294920 | tf_op jit(solution)/shard_map/ppermute | solution.py:402
  56.9 2.6 %collective-permute-start.12 = (bf16[192,256]{1,0:T(8,128)(2,1)S(1)}, bf16[192,256]{1,0:T(8,128)(2,1)S(1)}, u32[]{:S(2)}, u32[]{:S(2)}) collective-permute-start(bf16[192,256]{1,0:T(8,128)(2,1)S(1)} %get-tuple-element.52), channel_id=1, source_target_pairs={{0,8},{2,10},{4,12},{6,14},{8,0},{10,2},{12,4},{14,6},{1,9},{3,11}... | collective-permute-start | bytes 294920 | tf_op jit(solution)/shard_map/ppermute | solution.py:402
  59.4 0.7 collective-permute-start.13
  60.1 1.7 %collective-permute-start.9 = (bf16[752,256]{1,0:T(8,128)(2,1)S(1)}, bf16[752,256]{1,0:T(8,128)(2,1)S(1)}, u32[]{:S(2)}, u32[]{:S(2)}) collective-permute-start(bf16[752,256]{1,0:T(8,128)(2,1)S(1)} %get-tuple-element.47), channel_id=1, source_target_pairs={{0,2},{2,0},{4,6},{6,4},{8,10},{10,8},{12,14},{14,12},{1,3},{3,1},... | collective-permute-start | bytes 1155080 | tf_op jit(solution)/shard_map/ppermute | solution.py:384
  61.8 0.8 collective-permute-done.12.refs_2_
  62.6 4.7 %collective-permute-done.13.refs_3_ = bf16[192,256]{1,0:T(8,128)(2,1)S(1)} collective-permute-done((bf16[192,256]{1,0:T(8,128)(2,1)S(1)}, bf16[192,256]{1,0:T(8,128)(2,1)S(1)}, u32[]{:S(2)}, u32[]{:S(2)}) %collective-permute-start.13) | collective-permute-done | bytes 98336 | tf_op jit(solution)/shard_map/ppermute | solution.py:402
  67.3 0.7 collective-permute-start.14
  68.0 0.6 shard_map.116.refs_3_
  68.6 4.7 %collective-permute-start.15 = (bf16[192,256]{1,0:T(8,128)(2,1)S(1)}, bf16[192,256]{1,0:T(8,128)(2,1)S(1)}, u32[]{:S(2)}, u32[]{:S(2)}) collective-permute-start(bf16[192,256]{1,0:T(8,128)(2,1)S(1)} %shard_map.116.refs_3_), channel_id=1, source_target_pairs={{0,2},{2,0},{4,6},{6,4},{8,10},{10,8},{12,14},{14,12},{1,3},{3,1},... | collective-permute-start | bytes 294920 | tf_op jit(solution)/shard_map/ppermute | solution.py:417
  73.3 0.0 collective-permute-done.4.refs_3_
  73.3 3.9 %shard_map.109 = (bf16[4,720,256]{2,1,0:T(8,128)(2,1)}, f32[8,128]{1,0:T(8,128)S(1)}) custom-call(s32[6]{0:T(128)S(1)} %stack.23.info_ref.refs_0_, bf16[4,752,256]{2,1,0:T(8,128)(2,1)S(1)} %get-tuple-element.36.refs_1_.refs_7_.refs_9_, bf16[768,256]{1,0:T(8,128)(2,1)S(1)} %bitcast.16, bf16[752,256]{1,0:T(8,128)(2,1)S(1)} %collective-permute-done.4.refs_3_, ...), custom_call_target="tpu_custom_call" | custom-call | flops 2194145280 | bytes 11796480 | tf_op jit(solution)/shard_map/pallas_call | solution.py:249
  77.2 2.6 %collective-permute-done.9.refs_3_.refs_1_ = bf16[752,256]{1,0:T(8,128)(2,1)S(1)} collective-permute-done((bf16[752,256]{1,0:T(8,128)(2,1)S(1)}, bf16[752,256]{1,0:T(8,128)(2,1)S(1)}, u32[]{:S(2)}, u32[]{:S(2)}) %collective-permute-start.9) | collective-permute-done | bytes 385056 | tf_op jit(solution)/shard_map/ppermute | solution.py:384
  79.9 2.0 %collective-permute-done.15.refs_4_ = bf16[192,256]{1,0:T(8,128)(2,1)S(1)} collective-permute-done((bf16[192,256]{1,0:T(8,128)(2,1)S(1)}, bf16[192,256]{1,0:T(8,128)(2,1)S(1)}, u32[]{:S(2)}, u32[]{:S(2)}) %collective-permute-start.15) | collective-permute-done | bytes 98336 | tf_op jit(solution)/shard_map/ppermute | solution.py:417
  81.9 0.6 shard_map.117.refs_0_
  82.5 3.0 %collective-permute-start.16 = (bf16[192,256]{1,0:T(8,128)(2,1)S(1)}, bf16[192,256]{1,0:T(8,128)(2,1)S(1)}, u32[]{:S(2)}, u32[]{:S(2)}) collective-permute-start(bf16[192,256]{1,0:T(8,128)(2,1)S(1)} %shard_map.117.refs_0_), channel_id=1, source_target_pairs={{0,4},{2,6},{4,0},{6,2},{8,12},{10,14},{12,8},{14,10},{1,5},{3,7},... | collective-permute-start | bytes 294920 | tf_op jit(solution)/shard_map/ppermute | solution.py:402
  85.4 2.3 %collective-permute-start.17 = (bf16[192,256]{1,0:T(8,128)(2,1)S(1)}, bf16[192,256]{1,0:T(8,128)(2,1)S(1)}, u32[]{:S(2)}, u32[]{:S(2)}) collective-permute-start(bf16[192,256]{1,0:T(8,128)(2,1)S(1)} %shard_map.117.refs_0_), channel_id=1, source_target_pairs={{0,8},{2,10},{4,12},{6,14},{8,0},{10,2},{12,4},{14,6},{1,9},{3,11}... | collective-permute-start | bytes 294920 | tf_op jit(solution)/shard_map/ppermute | solution.py:402
  87.8 1.0 %collective-permute-start.18 = (bf16[192,256]{1,0:T(8,128)(2,1)S(1)}, bf16[192,256]{1,0:T(8,128)(2,1)S(1)}, u32[]{:S(2)}, u32[]{:S(2)}) collective-permute-start(bf16[192,256]{1,0:T(8,128)(2,1)S(1)} %shard_map.117.refs_0_), channel_id=1, source_target_pairs={{0,12},{2,14},{4,8},{6,10},{8,4},{10,6},{12,0},{14,2},{1,13},{3,15... | collective-permute-start | bytes 294920 | tf_op jit(solution)/shard_map/ppermute | solution.py:402
  88.8 4.1 %shard_map.115 = (bf16[4,720,256]{2,1,0:T(8,128)(2,1)}, f32[8,128]{1,0:T(8,128)}) custom-call(s32[6]{0:T(128)S(1)} %stack.23.info_ref.refs_0_, bf16[4,752,256]{2,1,0:T(8,128)(2,1)S(1)} %get-tuple-element.46.refs_1_, bf16[768,256]{1,0:T(8,128)(2,1)S(1)} %bitcast.18, bf16[752,256]{1,0:T(8,128)(2,1)S(1)} %collective-permute-done.9.refs_3_.refs_1_, ...), custom_call_target="tpu_custom_call" | custom-call | flops 2194145280 | bytes 11796480 | tf_op jit(solution)/shard_map/pallas_call | solution.py:249
  92.9 0.0 collective-permute-done.16.refs_1_
  92.9 2.9 %collective-permute-done.18.refs_3_ = bf16[192,256]{1,0:T(8,128)(2,1)S(1)} collective-permute-done((bf16[192,256]{1,0:T(8,128)(2,1)S(1)}, bf16[192,256]{1,0:T(8,128)(2,1)S(1)}, u32[]{:S(2)}, u32[]{:S(2)}) %collective-permute-start.18) | collective-permute-done | bytes 98336 | tf_op jit(solution)/shard_map/ppermute | solution.py:402
  95.8 0.5 collective-permute-start.20
  96.3 0.0 collective-permute-start.21
  96.3 0.5 collective-permute-start.22
  96.8 0.3 collective-permute-done.19.refs_4_
  97.1 0.2 collective-permute-done.20.refs_5_
  97.3 0.4 collective-permute-done.21.refs_6_
  97.6 0.2 collective-permute-done.22.refs_7_
  97.8 1.8 %shard_map.118 = (f32[768,256]{1,0:T(8,128)}, f32[768,256]{1,0:T(8,128)}) custom-call(s32[6]{0:T(128)S(1)} %stack.23.info_ref.refs_0_, bf16[192,256]{1,0:T(8,128)(2,1)S(1)} %shard_map.117.refs_0_, bf16[192,256]{1,0:T(8,128)(2,1)S(1)} %collective-permute-done.16.refs_1_, bf16[192,256]{1,0:T(8,128)(2,1)S(1)} %collective-permute-done.17.refs_2_, ...), custom_call_target="tpu_custom_call" | custom-call | flops 1 | bytes 1 | tf_op jit(solution)/shard_map/pallas_call | solution.py:299
  (29 shorter events, 0.1 us)
Async XLA Ops:
  0.6 7.4 %copy-start.1 = (bf16[4,720,256]{2,1,0:T(8,128)(2,1)S(1)}, bf16[4,720,256]{2,1,0:T(8,128)(2,1)}, u32[]{:S(2)}) copy-start(bf16[4,720,256]{2,1,0:T(8,128)(2,1)} %refs_1_) | copy-start | bytes 4423684
  0.6 8.0 %copy-start = (bf16[4,720,256]{2,1,0:T(8,128)(2,1)S(1)}, bf16[4,720,256]{2,1,0:T(8,128)(2,1)}, u32[]{:S(2)}) copy-start(bf16[4,720,256]{2,1,0:T(8,128)(2,1)} %refs_1_.2) | copy-start | bytes 4423684
  3.5 20.2 %collective-permute-start = (bf16[720,256]{1,0:T(8,128)(2,1)}, bf16[720,256]{1,0:T(8,128)(2,1)S(1)}, u32[]{:S(2)}, u32[]{:S(2)}) collective-permute-start(bf16[720,256]{1,0:T(8,128)(2,1)} %get-tuple-element.65), channel_id=1, source_target_pairs={{0,2},{2,0},{4,6},{6,4},{8,10},{10,8},{12,14},{14,12},{1,3},{3,1},... | collective-permute-start | bytes 1105928 | tf_op jit(solution)/shard_map/ppermute | solution.py:384
  6.5 17.2 %collective-permute-start.1 = (bf16[720,256]{1,0:T(8,128)(2,1)}, bf16[720,256]{1,0:T(8,128)(2,1)}, u32[]{:S(2)}, u32[]{:S(2)}) collective-permute-start(bf16[720,256]{1,0:T(8,128)(2,1)} %get-tuple-element.64), channel_id=1, source_target_pairs={{2,4},{4,2},{6,8},{8,6},{10,12},{12,10},{3,5},{5,3},{7,9},{9,7},{1... | collective-permute-start | bytes 1105928 | tf_op jit(solution)/shard_map/ppermute | solution.py:388
  8.0 1.8 %copy-start.5 = (s32[4]{0:T(128)S(1)}, s32[4]{0:T(128)}, u32[]{:S(2)}) copy-start(s32[4]{0:T(128)} %param.9) | copy-start | bytes 52
  8.0 1.8 %copy-start.4 = (bf16[4,3,3,17]{3,0,2,1:T(4,128)(2,1)S(1)}, bf16[4,3,3,17]{3,0,2,1:T(4,128)(2,1)}, u32[]{:S(2)}) copy-start(bf16[4,3,3,17]{3,0,2,1:T(4,128)(2,1)} %param.10) | copy-start | bytes 3676
  8.6 16.6 %collective-permute-start.2 = (bf16[4,32,256]{2,1,0:T(8,128)(2,1)S(1)}, bf16[4,32,256]{2,1,0:T(8,128)(2,1)}, u32[]{:S(2)}, u32[]{:S(2)}) collective-permute-start(bf16[4,32,256]{2,1,0:T(8,128)(2,1)S(1)} %shard_map.102), channel_id=1, source_target_pairs={{0,1},{1,0},{2,3},{3,2},{4,5},{5,4},{6,7},{7,6},{8,9},{9,8},{10,11... | collective-permute-start | bytes 196616 | tf_op jit(solution)/shard_map/ppermute | solution.py:396
  9.2 1.5 %collective-permute-start.5 = (bf16[4,32,256]{2,1,0:T(8,128)(2,1)S(1)}, bf16[4,32,256]{2,1,0:T(8,128)(2,1)S(1)}, u32[]{:S(2)}, u32[]{:S(2)}) collective-permute-start(bf16[4,32,256]{2,1,0:T(8,128)(2,1)S(1)} %shard_map.104), channel_id=1, source_target_pairs={{0,1},{1,0},{2,3},{3,2},{4,5},{5,4},{6,7},{7,6},{8,9},{9,8},{10,11... | collective-permute-start | bytes 196616 | tf_op jit(solution)/shard_map/ppermute | solution.py:396
  11.4 15.0 %copy-start.3 = (bf16[3,256,256]{2,1,0:T(8,128)(2,1)S(1)}, bf16[3,256,256]{2,1,0:T(8,128)(2,1)}, u32[]{:S(2)}) copy-start(bf16[3,256,256]{2,1,0:T(8,128)(2,1)} %param.11) | copy-start | bytes 1179652
  11.4 27.9 %collective-permute-start.6 = (bf16[768,256]{1,0:T(8,128)(2,1)S(1)}, bf16[768,256]{1,0:T(8,128)(2,1)S(1)}, u32[]{:S(2)}, u32[]{:S(2)}) collective-permute-start(bf16[768,256]{1,0:T(8,128)(2,1)S(1)} %shard_map.105), channel_id=1, source_target_pairs={{0,2},{2,0},{4,6},{6,4},{8,10},{10,8},{12,14},{14,12},{1,3},{3,1},... | collective-permute-start | bytes 1179656 | tf_op jit(solution)/shard_map/ppermute | solution.py:384
  23.7 15.6 %collective-permute-start.7 = (bf16[768,256]{1,0:T(8,128)(2,1)S(1)}, bf16[768,256]{1,0:T(8,128)(2,1)S(1)}, u32[]{:S(2)}, u32[]{:S(2)}) collective-permute-start(bf16[768,256]{1,0:T(8,128)(2,1)S(1)} %shard_map.107), channel_id=1, source_target_pairs={{2,4},{4,2},{6,8},{8,6},{10,12},{12,10},{3,5},{5,3},{7,9},{9,7},{1... | collective-permute-start | bytes 1179656 | tf_op jit(solution)/shard_map/ppermute | solution.py:388
  25.1 1.2 %collective-permute-start.3 = (bf16[64,256]{1,0:T(8,128)(2,1)S(1)}, bf16[64,256]{1,0:T(8,128)(2,1)S(1)}, u32[]{:S(2)}, u32[]{:S(2)}) collective-permute-start(bf16[64,256]{1,0:T(8,128)(2,1)S(1)} %pad_maximum_fusion), channel_id=1, source_target_pairs={{0,1},{1,0},{2,3},{3,2},{4,5},{5,4},{6,7},{7,6},{8,9},{9,8},{10,11... | collective-permute-start | bytes 98312 | tf_op jit(solution)/shard_map/ppermute | solution.py:396
  26.3 3.4 %copy-start.2 = (bf16[3,256,256]{2,1,0:T(8,128)(2,1)S(1)}, bf16[3,256,256]{2,1,0:T(8,128)(2,1)}, u32[]{:S(2)}) copy-start(bf16[3,256,256]{2,1,0:T(8,128)(2,1)} %param.12) | copy-start | bytes 1179652
  39.3 5.5 %collective-permute-start.8 = (bf16[752,256]{1,0:T(8,128)(2,1)S(1)}, bf16[752,256]{1,0:T(8,128)(2,1)S(1)}, u32[]{:S(2)}, u32[]{:S(2)}) collective-permute-start(bf16[752,256]{1,0:T(8,128)(2,1)S(1)} %shard_map.108), channel_id=1, source_target_pairs={{2,4},{4,2},{6,8},{8,6},{10,12},{12,10},{3,5},{5,3},{7,9},{9,7},{1... | collective-permute-start | bytes 1155080 | tf_op jit(solution)/shard_map/ppermute | solution.py:388
  44.8 9.6 %collective-permute-start.10 = (bf16[768,256]{1,0:T(8,128)(2,1)S(1)}, bf16[768,256]{1,0:T(8,128)(2,1)S(1)}, u32[]{:S(2)}, u32[]{:S(2)}) collective-permute-start(bf16[768,256]{1,0:T(8,128)(2,1)S(1)} %shard_map.112), channel_id=1, source_target_pairs={{0,1},{1,0},{2,3},{3,2},{4,5},{5,4},{6,7},{7,6},{8,9},{9,8},{10,11... | collective-permute-start | bytes 1179656 | tf_op jit(solution)/shard_map/ppermute | solution.py:396
  44.9 28.4 %collective-permute-start.4 = (bf16[752,256]{1,0:T(8,128)(2,1)S(1)}, bf16[752,256]{1,0:T(8,128)(2,1)S(1)}, u32[]{:S(2)}, u32[]{:S(2)}) collective-permute-start(bf16[752,256]{1,0:T(8,128)(2,1)S(1)} %get-tuple-element.37), channel_id=1, source_target_pairs={{0,2},{2,0},{4,6},{6,4},{8,10},{10,8},{12,14},{14,12},{1,3},{3,1},... | collective-permute-start | bytes 1155080 | tf_op jit(solution)/shard_map/ppermute | solution.py:384
  55.0 6.8 %collective-permute-start.11 = (bf16[192,256]{1,0:T(8,128)(2,1)S(1)}, bf16[192,256]{1,0:T(8,128)(2,1)S(1)}, u32[]{:S(2)}, u32[]{:S(2)}) collective-permute-start(bf16[192,256]{1,0:T(8,128)(2,1)S(1)} %get-tuple-element.51), channel_id=1, source_target_pairs={{0,4},{2,6},{4,0},{6,2},{8,12},{10,14},{12,8},{14,10},{1,5},{3,7},... | collective-permute-start | bytes 294920 | tf_op jit(solution)/shard_map/ppermute | solution.py:402
  56.9 5.8 %collective-permute-start.12 = (bf16[192,256]{1,0:T(8,128)(2,1)S(1)}, bf16[192,256]{1,0:T(8,128)(2,1)S(1)}, u32[]{:S(2)}, u32[]{:S(2)}) collective-permute-start(bf16[192,256]{1,0:T(8,128)(2,1)S(1)} %get-tuple-element.52), channel_id=1, source_target_pairs={{0,8},{2,10},{4,12},{6,14},{8,0},{10,2},{12,4},{14,6},{1,9},{3,11}... | collective-permute-start | bytes 294920 | tf_op jit(solution)/shard_map/ppermute | solution.py:402
  59.4 7.9 %collective-permute-start.13 = (bf16[192,256]{1,0:T(8,128)(2,1)S(1)}, bf16[192,256]{1,0:T(8,128)(2,1)S(1)}, u32[]{:S(2)}, u32[]{:S(2)}) collective-permute-start(bf16[192,256]{1,0:T(8,128)(2,1)S(1)} %get-tuple-element.53), channel_id=1, source_target_pairs={{0,12},{2,14},{4,8},{6,10},{8,4},{10,6},{12,0},{14,2},{1,13},{3,15... | collective-permute-start | bytes 294920 | tf_op jit(solution)/shard_map/ppermute | solution.py:402
  60.1 19.7 %collective-permute-start.9 = (bf16[752,256]{1,0:T(8,128)(2,1)S(1)}, bf16[752,256]{1,0:T(8,128)(2,1)S(1)}, u32[]{:S(2)}, u32[]{:S(2)}) collective-permute-start(bf16[752,256]{1,0:T(8,128)(2,1)S(1)} %get-tuple-element.47), channel_id=1, source_target_pairs={{0,2},{2,0},{4,6},{6,4},{8,10},{10,8},{12,14},{14,12},{1,3},{3,1},... | collective-permute-start | bytes 1155080 | tf_op jit(solution)/shard_map/ppermute | solution.py:384
  67.3 14.5 %collective-permute-start.14 = (bf16[752,256]{1,0:T(8,128)(2,1)S(1)}, bf16[752,256]{1,0:T(8,128)(2,1)S(1)}, u32[]{:S(2)}, u32[]{:S(2)}) collective-permute-start(bf16[752,256]{1,0:T(8,128)(2,1)S(1)} %shard_map.114), channel_id=1, source_target_pairs={{2,4},{4,2},{6,8},{8,6},{10,12},{12,10},{3,5},{5,3},{7,9},{9,7},{1... | collective-permute-start | bytes 1155080 | tf_op jit(solution)/shard_map/ppermute | solution.py:388
  68.6 13.3 %collective-permute-start.15 = (bf16[192,256]{1,0:T(8,128)(2,1)S(1)}, bf16[192,256]{1,0:T(8,128)(2,1)S(1)}, u32[]{:S(2)}, u32[]{:S(2)}) collective-permute-start(bf16[192,256]{1,0:T(8,128)(2,1)S(1)} %shard_map.116.refs_3_), channel_id=1, source_target_pairs={{0,2},{2,0},{4,6},{6,4},{8,10},{10,8},{12,14},{14,12},{1,3},{3,1},... | collective-permute-start | bytes 294920 | tf_op jit(solution)/shard_map/ppermute | solution.py:417
  82.5 10.5 %collective-permute-start.16 = (bf16[192,256]{1,0:T(8,128)(2,1)S(1)}, bf16[192,256]{1,0:T(8,128)(2,1)S(1)}, u32[]{:S(2)}, u32[]{:S(2)}) collective-permute-start(bf16[192,256]{1,0:T(8,128)(2,1)S(1)} %shard_map.117.refs_0_), channel_id=1, source_target_pairs={{0,4},{2,6},{4,0},{6,2},{8,12},{10,14},{12,8},{14,10},{1,5},{3,7},... | collective-permute-start | bytes 294920 | tf_op jit(solution)/shard_map/ppermute | solution.py:402
  85.4 7.5 %collective-permute-start.17 = (bf16[192,256]{1,0:T(8,128)(2,1)S(1)}, bf16[192,256]{1,0:T(8,128)(2,1)S(1)}, u32[]{:S(2)}, u32[]{:S(2)}) collective-permute-start(bf16[192,256]{1,0:T(8,128)(2,1)S(1)} %shard_map.117.refs_0_), channel_id=1, source_target_pairs={{0,8},{2,10},{4,12},{6,14},{8,0},{10,2},{12,4},{14,6},{1,9},{3,11}... | collective-permute-start | bytes 294920 | tf_op jit(solution)/shard_map/ppermute | solution.py:402
  87.8 8.1 %collective-permute-start.18 = (bf16[192,256]{1,0:T(8,128)(2,1)S(1)}, bf16[192,256]{1,0:T(8,128)(2,1)S(1)}, u32[]{:S(2)}, u32[]{:S(2)}) collective-permute-start(bf16[192,256]{1,0:T(8,128)(2,1)S(1)} %shard_map.117.refs_0_), channel_id=1, source_target_pairs={{0,12},{2,14},{4,8},{6,10},{8,4},{10,6},{12,0},{14,2},{1,13},{3,15... | collective-permute-start | bytes 294920 | tf_op jit(solution)/shard_map/ppermute | solution.py:402
  95.8 1.3 %collective-permute-start.19 = (bf16[192,256]{1,0:T(8,128)(2,1)S(1)}, bf16[192,256]{1,0:T(8,128)(2,1)S(1)}, u32[]{:S(2)}, u32[]{:S(2)}) collective-permute-start(bf16[192,256]{1,0:T(8,128)(2,1)S(1)} %shard_map.117.refs_0_), channel_id=1, source_target_pairs={{0,1},{1,0},{2,3},{3,2},{4,5},{5,4},{6,7},{7,6},{8,9},{9,8},{10,11... | collective-permute-start | bytes 294920 | tf_op jit(solution)/shard_map/ppermute | solution.py:396
  95.8 1.5 %collective-permute-start.20 = (bf16[192,256]{1,0:T(8,128)(2,1)S(1)}, bf16[192,256]{1,0:T(8,128)(2,1)S(1)}, u32[]{:S(2)}, u32[]{:S(2)}) collective-permute-start(bf16[192,256]{1,0:T(8,128)(2,1)S(1)} %collective-permute-done.16.refs_1_), channel_id=1, source_target_pairs={{0,1},{1,0},{2,3},{3,2},{4,5},{5,4},{6,7},{7,6},{8,9},{9,8},{10,11... | collective-permute-start | bytes 294920 | tf_op jit(solution)/shard_map/ppermute | solution.py:396
  96.3 1.3 %collective-permute-start.21 = (bf16[192,256]{1,0:T(8,128)(2,1)S(1)}, bf16[192,256]{1,0:T(8,128)(2,1)S(1)}, u32[]{:S(2)}, u32[]{:S(2)}) collective-permute-start(bf16[192,256]{1,0:T(8,128)(2,1)S(1)} %collective-permute-done.17.refs_2_), channel_id=1, source_target_pairs={{0,1},{1,0},{2,3},{3,2},{4,5},{5,4},{6,7},{7,6},{8,9},{9,8},{10,11... | collective-permute-start | bytes 294920 | tf_op jit(solution)/shard_map/ppermute | solution.py:396
  96.3 1.5 %collective-permute-start.22 = (bf16[192,256]{1,0:T(8,128)(2,1)S(1)}, bf16[192,256]{1,0:T(8,128)(2,1)S(1)}, u32[]{:S(2)}, u32[]{:S(2)}) collective-permute-start(bf16[192,256]{1,0:T(8,128)(2,1)S(1)} %collective-permute-done.18.refs_3_), channel_id=1, source_target_pairs={{0,1},{1,0},{2,3},{3,2},{4,5},{5,4},{6,7},{7,6},{8,9},{9,8},{10,11... | collective-permute-start | bytes 294920 | tf_op jit(solution)/shard_map/ppermute | solution.py:396
